TPU v7x, 512 devices: a whole 4x8x8 slice. The times are simulated.
512 devices in a mesh: ys: 16 (over z_lo, x), xs: 32 (over y, z_hi, core).
Axes of the slice: x: 4, y: 8, z: 8 (z_hi: 2, z_lo: 4; z = z_hi * 4 + z_lo), core: 2. Of those that a mesh axis runs over, the one named last changes fastest.
Arguments:
- forward_u: float32 [48, 128, 1024], P(None, 'ys', 'xs'), may hold values from -6 to 6
- forward_v: float32 [48, 128, 1024], P(None, 'ys', 'xs'), may hold values from -6 to 6
- forward_w: float32 [48, 128, 1024], P(None, 'ys', 'xs'), may hold values from -6 to 6
- forward_tracer: float32 [48, 128, 1024], P(None, 'ys', 'xs'), may hold values from -6 to 6
- incoming_u: float32 [48, 128, 1024], P(None, 'ys', 'xs'), may hold values from -6 to 6
- incoming_v: float32 [48, 128, 1024], P(None, 'ys', 'xs'), may hold values from -6 to 6
- incoming_w: float32 [48, 128, 1024], P(None, 'ys', 'xs'), may hold values from -6 to 6
- incoming_tracer: float32 [48, 128, 1024], P(None, 'ys', 'xs'), may hold values from -6 to 6
- diffusion_inverse: float32 [48, 48], replicated, may hold values from -1.5 to 2.5, as said below
- mode_vectors: float32 [48, 48], replicated, may hold values from -1.5 to 2.5, as said below
- mode_inverse: float32 [48, 48], replicated, may hold values from -1.5 to 2.5, as said below
- mode_eigen: float32 [48], replicated, may hold values from 0.0003 to 4
Outputs:
- adjoint_u: float32 [48, 128, 1024], P(None, 'ys', 'xs')
- adjoint_v: float32 [48, 128, 1024], P(None, 'ys', 'xs')
- adjoint_w: float32 [48, 128, 1024], P(None, 'ys', 'xs')
- adjoint_tracer: float32 [48, 128, 1024], P(None, 'ys', 'xs')
Inputs may be any that keep to these rules, and one draw needn't show every extreme that they name: `diffusion_inverse`: a given 48 x 48 matrix. `mode_vectors`: a given 48 x 48 matrix. `mode_inverse`: a given 48 x 48 matrix.
All inputs are finite; a program needn't handle non-finite values.
Results may differ from a plain program's by a relative error of at most 0.0003.
Values sent between devices are 32-bit elements; how exact they have to be, the bound alone decides.
A program may use at most 64 MiB of HBM per device.

v0:
```python
import functools

import jax
import jax.numpy as jnp
import numpy as np
from jax import lax
from jax.experimental import pallas as pl
from jax.experimental.pallas import tpu as pltpu
from jax.sharding import PartitionSpec as P

MESH = pl.DeviceIdType.MESH
DT = 0.25
NU = 0.1
KAPPA = 0.1
GRAV = 1.0
EPS = 1e-6
F32 = jnp.float32
HI = lax.Precision.HIGHEST
ROWS, COLS = 8, 32


def tables(ns, nt):
    nx, ny = COLS * nt, ROWS * ns
    t = np.arange(nt)
    ring = np.zeros((2, ns, nt))
    ring[0, 0] = 1 / np.sqrt(nt)
    ring[1, 0] = (-1.0) ** t / np.sqrt(nt)
    for j in range(1, ns):
        ring[0, j] = np.sqrt(2 / nt) * np.cos(2 * np.pi * j * t / nt)
        ring[1, j] = np.sqrt(2 / nt) * np.sin(2 * np.pi * j * t / nt)

    def basis(n, k):
        z = np.arange(n)
        if k == 0 or 2 * k == n:
            return [np.cos(2 * np.pi * k * z / n) / np.sqrt(n)]
        return [
            np.sqrt(2 / n) * np.cos(2 * np.pi * k * z / n),
            np.sqrt(2 / n) * np.sin(2 * np.pi * k * z / n),
        ]

    inner = np.zeros((ns, 2, 2, COLS, 2, 2, COLS))
    lamx = np.zeros((ns, 2, 2, COLS))
    for j in range(ns):
        found, lam = [], []
        for k in range(nx // 2 + 1):
            res = k % nt
            own = res in (0, nt // 2) if j == 0 else res in (j, nt - j)
            if own:
                for vec in basis(nx, k):
                    found.append(np.einsum("qt,tc->qc", ring[:, j], vec.reshape(nt, COLS)))
                    lam.append(4 * np.sin(np.pi * k / nx) ** 2)
        block = np.stack(found, -1).reshape(2, COLS, 2, COLS)
        for m in range(2):
            inner[j, :, m, :, :, m, :] = block
            lamx[j, :, m, :] = np.array(lam).reshape(2, COLS)
    inner = inner.reshape(ns, 4 * COLS, 4 * COLS)
    lamx = np.broadcast_to(lamx.reshape(ns, 1, 4 * COLS), (ns, 8, 4 * COLS))
    spectral = np.concatenate([inner, lamx], 1)

    ybase, ylam = [], []
    for k in range(ny // 2 + 1):
        for vec in basis(ny, k):
            ybase.append(vec)
            ylam.append(4 * np.sin(np.pi * k / ny) ** 2)
    ybase = np.stack(ybase)
    lamy = np.broadcast_to(np.array(ylam)[:, None], (ny, 128))
    yfwd = ybase.reshape(ny, ns, 4, 2).transpose(0, 3, 2, 1).reshape(ny, ny)
    yinv = np.zeros((ns, 16, ny))
    for s in range(ns):
        for r in range(14):
            yinv[s, r] = ybase[:, (ROWS * s - 3 + r) % ny]
    yinv = yinv.reshape(16 * ns, ny)
    ring = ring.reshape(nt, nt)
    out = (ring, ring.T, yfwd, yinv, spectral, lamy)
    return tuple(np.ascontiguousarray(v).astype(np.float32) for v in out)


def dot(a, b):
    return lax.dot_general(a, b, (((1,), (0,)), ((), ())), precision=HI, preferred_element_type=F32)


def dot_tn(a, b):
    return lax.dot_general(a, b, (((0,), (0,)), ((), ())), precision=HI, preferred_element_type=F32)


def dot_nt(a, b):
    return lax.dot_general(a, b, (((1,), (1,)), ((), ())), precision=HI, preferred_element_type=F32)


def roll(v, shift, axis=1):
    shift = shift % v.shape[axis]
    return v if shift == 0 else pltpu.roll(v, shift, axis)


def weno_parts(c, u, step, cut):
    stencil = [cut(roll(c, -k * step)) for k in range(-2, 4)]
    pos = u >= 0.0
    a = jnp.where(pos, stencil[0], stencil[5])
    b = jnp.where(pos, stencil[1], stencil[4])
    m = jnp.where(pos, stencil[2], stencil[3])
    p = jnp.where(pos, stencil[3], stencil[2])
    q = jnp.where(pos, stencil[4], stencil[1])
    e0, f0 = a - 2.0 * b + m, a - 4.0 * b + 3.0 * m
    e1, f1 = b - 2.0 * m + p, b - p
    e2, f2 = m - 2.0 * p + q, 3.0 * m - 4.0 * p + q
    r0 = 1.0 / (EPS + (13.0 / 12.0 * e0 * e0 + 0.25 * f0 * f0))
    r1 = 1.0 / (EPS + (13.0 / 12.0 * e1 * e1 + 0.25 * f1 * f1))
    r2 = 1.0 / (EPS + (13.0 / 12.0 * e2 * e2 + 0.25 * f2 * f2))
    w0, w1, w2 = 0.1 * r0 * r0, 0.6 * r1 * r1, 0.3 * r2 * r2
    inv = 1.0 / (w0 + w1 + w2)
    w0, w1, w2 = w0 * inv, w1 * inv, w2 * inv
    v0 = (2.0 * a - 7.0 * b + 11.0 * m) * (1.0 / 6.0)
    v1 = (5.0 * m - b + 2.0 * p) * (1.0 / 6.0)
    v2 = (2.0 * m + 5.0 * p - q) * (1.0 / 6.0)
    value = w0 * v0 + w1 * v1 + w2 * v2
    w0, w1, w2 = w0 * u, w1 * u, w2 * u
    h0 = -2.0 * w0 * r0 * (v0 - value)
    h1 = -2.0 * w1 * r1 * (v1 - value)
    h2 = -2.0 * w2 * r2 * (v2 - value)
    e0, f0 = h0 * e0 * (13.0 / 6.0), h0 * f0 * 0.5
    e1, f1 = h1 * e1 * (13.0 / 6.0), h1 * f1 * 0.5
    e2, f2 = h2 * e2 * (13.0 / 6.0), h2 * f2 * 0.5
    w0, w1, w2 = w0 * (1.0 / 6.0), w1 * (1.0 / 6.0), w2 * (1.0 / 6.0)
    ga = 2.0 * w0 + e0 + f0
    gb = -7.0 * w0 - w1 - 2.0 * e0 - 4.0 * f0 + e1 + f1
    gm = 11.0 * w0 + 5.0 * w1 + 2.0 * w2 + e0 + 3.0 * f0 - 2.0 * e1 + e2 + 3.0 * f2
    gp = 2.0 * w1 + 5.0 * w2 + e1 - f1 - 2.0 * e2 - 4.0 * f2
    gq = e2 + f2 - w2
    zero = jnp.zeros_like(ga)
    return value, (
        jnp.where(pos, ga, zero),
        jnp.where(pos, gb, gq),
        jnp.where(pos, gm, gp),
        jnp.where(pos, gp, gm),
        jnp.where(pos, gq, gb),
        jnp.where(pos, zero, ga),
    )


def spread(f):
    return roll(f, 1) + roll(f, -1) + roll(f, 64) + roll(f, -64) - 4.0 * f


def kernel(
    ns, nt, nz,
    fu_h, fv_h, fw_h, fc_h, iu_h, iv_h, iw_h, it_h, dinv, vecs, minv, eig, ring, ring_t, yfwd, yinv, spec_h, lamy,
    out_u, out_v, out_w, out_c,
    raw, spec, u10, v14, w10, c18, iu10, iv10, iw14, it14, modal,
    xe, xw, xfw, xfe, yn1, ys1, yfs1, yfn1, yn2, ys2, yfs2, yfn2,
    s1, r1, s2, r2, s3, r3, s4, r4,
    ax, wx, ay, wy, ch, d_buf, p_buf, mw_buf, ou, ov, ow, oc,
    in_sem, h_send, h_recv, p_send, p_recv,
):
    ng = nz // 2
    s, t = lax.axis_index("ys"), lax.axis_index("xs")
    owner = t < ng

    loads = []
    for n, src in enumerate((iu_h, iv_h, iw_h, it_h, fc_h, fu_h, fv_h, fw_h)):
        loads.append(pltpu.make_async_copy(src, raw.at[n], in_sem.at[n]))
    loads.append(pltpu.make_async_copy(spec_h.at[s], spec, in_sem.at[8]))
    for copy in loads:
        copy.start()

    barrier = pltpu.get_barrier_semaphore()

    def greet_x(i, _):
        pl.semaphore_signal(barrier, 1, device_id=(s, lax.rem(t + i, nt)), device_id_type=MESH)
        return 0

    def greet_y(i, _):
        pl.semaphore_signal(barrier, 1, device_id=(lax.rem(s + i, ns), t), device_id_type=MESH)
        return 0

    lax.fori_loop(1, nt, greet_x, 0)
    lax.fori_loop(1, ns, greet_y, 0)

    lane = lax.broadcasted_iota(jnp.int32, (nz, 128), 1)
    slot = lane & 63
    low = lane < 64
    core = (slot >= 8) & (slot < 40)
    lane_g = lax.broadcasted_iota(jnp.int32, (ng, 128), 1)
    level = lax.broadcasted_iota(jnp.int32, (nz, 640), 0)

    def rows(n, count):
        return pl.ds(pl.multiple_of(n * count, count), count)

    def tile(n):
        return slice(128 * n, 128 * n + 128)

    def place(n, buf, first):
        loads[n].wait()
        for r in range(ROWS):
            at = 128 * first + 64 * (r + 1) + 8
            buf[:, at : at + COLS] = raw[n, pl.ds(r, nz, stride=ROWS), :]

    def pack_x(fields, out):
        total = jnp.zeros((nz, 128), F32)
        for buf, first, col, at, count in fields:
            for k in range(4):
                if k == 0:
                    v = jnp.where(low, buf[:, tile(first + 4)], buf[:, tile(first)])
                else:
                    v = buf[:, tile(first + k)]
                to = 16 * k + at
                total = jnp.where((slot >= to) & (slot < to + count), roll(v, to - 8 - col), total)
        out[...] = total

    def unpack_x(src, fields):
        v = src[...]
        for buf, first, col, at, count in fields:
            here = (slot >= 8 + col) & (slot < 8 + col + count)
            for k in range(4):
                w = roll(v, 8 + col - 16 * k - at)
                if k == 0:
                    z = tile(first + 4)
                    buf[:, z] = jnp.where(here & low, w, buf[:, z])
                    z = tile(first)
                    buf[:, z] = jnp.where(here & ~low, w, buf[:, z])
                else:
                    z = tile(first + k)
                    buf[:, z] = jnp.where(here, w, buf[:, z])

    def pair(one, two):
        return jnp.where(core, one, roll(two, 32))

    def remote(src, dst, ds, dt, send, recv):
        return pltpu.make_async_remote_copy(
            src_ref=src, dst_ref=dst, send_sem=send, recv_sem=recv, device_id=(ds, dt), device_id_type=MESH
        )

    east, west = lax.rem(t + 1, nt), lax.rem(t + nt - 1, nt)
    north, south = lax.rem(s + 1, ns), lax.rem(s + ns - 1, ns)

    place(0, iu10, 0)
    place(1, iv10, 0)
    pack_x(((iu10, 0, 31, 6, 1), (iv10, 0, 31, 7, 1)), xe.at[0])
    pack_x(((iu10, 0, 0, 6, 1), (iv10, 0, 0, 7, 1)), xw.at[0])
    yn1[...] = pair(iu10[:, tile(4)], iv10[:, tile(4)])
    ys1[...] = pair(iu10[:, tile(0)], iv10[:, tile(0)])

    pl.semaphore_wait(barrier, nt - 1 + ns - 1)
    first_halo = [
        remote(xe.at[0], xfw.at[0], s, east, h_send.at[0], h_recv.at[0]),
        remote(yn1, yfs1, north, t, h_send.at[1], h_recv.at[1]),
        remote(xw.at[0], xfe.at[0], s, west, h_send.at[2], h_recv.at[2]),
        remote(ys1, yfn1, south, t, h_send.at[3], h_recv.at[3]),
    ]
    for copy in first_halo:
        copy.start()

    place(2, iw14, 1)
    place(3, it14, 1)
    place(4, c18, 2)
    place(5, u10, 0)
    place(6, v14, 1)
    place(7, w10, 0)

    pack_x(((iw14, 1, 29, 0, 3), (it14, 1, 29, 3, 3), (u10, 0, 29, 8, 3), (c18, 2, 27, 11, 5)), xe.at[1])
    pack_x(((iw14, 1, 0, 0, 3), (it14, 1, 0, 3, 3), (u10, 0, 0, 8, 2), (c18, 2, 0, 11, 5)), xw.at[1])
    for n in range(3):
        yn2[n] = pair(c18[:, tile(4 + n)], v14[:, tile(3 + n)])
        ys2[n] = pair(c18[:, tile(2 + n)], v14[:, tile(1 + n)])
    for n in range(2):
        yn2[3 + n] = pair(iw14[:, tile(4 + n)], it14[:, tile(4 + n)])
        ys2[3 + n] = pair(iw14[:, tile(1 + n)], it14[:, tile(1 + n)])

    first_halo[0].wait_recv()
    unpack_x(xfw.at[0], ((iu10, 0, -1, 6, 1), (iv10, 0, -1, 7, 1)))
    first_halo[1].wait_recv()
    v = yfs1[...]
    iu10[:, tile(0)] = jnp.where(low, v, iu10[:, tile(0)])
    iv10[:, tile(0)] = jnp.where(low, roll(v, -32), iv10[:, tile(0)])

    iu, iv, iw = iu10[...], iv10[...], iw14[:, 128:768]
    below = jnp.where(level == 0, 0.0, roll(iw, 1, 0))
    div = iu - roll(iu, 1) + (iv - roll(iv, 64)) + (iw - below)
    div = roll(div, -64)[:, :512]
    div = dot_tn(vecs[...], div)
    half = (lane_g & 63) < 32
    for i in range(4):
        modal[i] = div[:, tile(i)]
        even = modal[i, pl.ds(0, ng, stride=2), :]
        odd = modal[i, pl.ds(1, ng, stride=2), :]
        s1[:, i, :] = jnp.where(half, roll(even, -8), roll(odd, 24))

    def send1(i, _):
        g = lax.rem(t + i, ng)

        @pl.when(g != t)
        def _():
            remote(s1.at[g], r1.at[t], s, g, p_send.at[0], p_recv.at[0]).start()

        return 0

    lax.fori_loop(0, ng, send1, 0)

    @pl.when(owner)
    def _():
        pltpu.make_async_copy(s1.at[t], r1.at[t], p_recv.at[0]).start()

    second_halo = [
        remote(xe.at[1], xfw.at[1], s, east, h_send.at[4], h_recv.at[4]),
        remote(yn2, yfs2, north, t, h_send.at[5], h_recv.at[5]),
        remote(xw.at[1], xfe.at[1], s, west, h_send.at[6], h_recv.at[6]),
        remote(ys2, yfn2, south, t, h_send.at[7], h_recv.at[7]),
    ]
    for copy in second_halo:
        copy.start()

    @pl.when(owner)
    def _():
        pltpu.make_async_copy(r1, r1, p_recv.at[0]).wait()
        x = jnp.concatenate([r1[:, i, :] for i in range(4)], 1)
        y = dot(ring[...], x)
        for q in range(2):
            for i in range(4):
                s2[pl.ds(4 * q + i, ns, stride=8), :] = y[q * ns : (q + 1) * ns, tile(i)]

        def send2(i, _):
            j = lax.rem(s + i, ns)
            remote(s2.at[rows(j, 8)], r2.at[rows(s, 8)], j, t, p_send.at[1], p_recv.at[1]).start()
            return 0

        lax.fori_loop(1, ns, send2, 0)
        pltpu.make_async_copy(s2.at[rows(s, 8)], r2.at[rows(s, 8)], p_recv.at[1]).start()

    first_halo[2].wait_recv()
    unpack_x(xfe.at[0], ((iu10, 0, 32, 6, 1), (iv10, 0, 32, 7, 1)))
    first_halo[3].wait_recv()
    v = yfn1[...]
    iu10[:, tile(4)] = jnp.where(low, iu10[:, tile(4)], v)
    iv10[:, tile(4)] = jnp.where(low, iv10[:, tile(4)], roll(v, -32))
    second_halo[0].wait_recv()
    unpack_x(xfw.at[1], ((iw14, 1, -3, 0, 3), (it14, 1, -3, 3, 3), (u10, 0, -3, 8, 3), (c18, 2, -5, 11, 5)))
    second_halo[2].wait_recv()
    unpack_x(xfe.at[1], ((iw14, 1, 32, 0, 3), (it14, 1, 32, 3, 3), (u10, 0, 32, 8, 2), (c18, 2, 32, 11, 5)))

    def x_faces(n, _):
        at = pl.ds(pl.multiple_of(8 * n, 8), 8)
        value, parts = weno_parts(c18[at, 256:896], u10[at, :], 1, lambda f: f)
        wx[at, :] = value
        for o in range(6):
            ax[o, at, :] = parts[o]
        return 0

    lax.fori_loop(0, nz // 8, x_faces, 0)

    @pl.when(owner)
    def _():
        loads[8].wait()
        pltpu.make_async_copy(r2, r2, p_recv.at[1]).wait()
        part = [
            jnp.concatenate([r2[pl.ds(4 * q + i, ns, stride=8), :] for i in range(4)], 0) for q in range(2)
        ]
        left = lax.broadcasted_iota(jnp.int32, (4 * ns, 128), 1) < 64
        x = jnp.concatenate(
            [
                jnp.where(left, part[0], roll(part[1], 64)),
                jnp.where(left, roll(part[0], 64), part[1]),
            ],
            0,
        )
        inner = spec[0:128, :]
        y = dot(dot(yfwd[...], x), inner)
        wide = lax.broadcasted_iota(jnp.int32, (1, 128), 1)
        own = jnp.where((wide & 32) == 0, eig[2 * t], eig[2 * t + 1])
        y = -y / (own + lamy[...] + spec[128:129, :])
        y = dot(yinv[...], dot_nt(y, inner))
        s3[...] = y

        def send3(i, _):
            j = lax.rem(s + i, ns)
            remote(s3.at[rows(j, 16)], r3.at[rows(s, 16)], j, t, p_send.at[2], p_recv.at[2]).start()
            return 0

        lax.fori_loop(1, ns, send3, 0)
        pltpu.make_async_copy(s3.at[rows(s, 16)], r3.at[rows(s, 16)], p_recv.at[2]).start()

    second_halo[1].wait_recv()
    second_halo[3].wait_recv()
    for n in range(3):
        v = yfs2[n]
        for buf, k, f in ((c18, n, v), (v14, n - 1, roll(v, -32))):
            if k >= 0:
                buf[:, tile(k)] = f if n < 2 else jnp.where(low, f, buf[:, tile(k)])
        v = yfn2[n]
        for buf, k, f in ((c18, 6 + n, v), (v14, 5 + n, roll(v, -32))):
            if k < buf.shape[1] // 128:
                buf[:, tile(k)] = f if n > 0 else jnp.where(low, buf[:, tile(k)], f)
    for n in range(2):
        v = yfs2[3 + n]
        for buf, f in ((iw14, v), (it14, roll(v, -32))):
            buf[:, tile(n)] = f if n < 1 else jnp.where(low, f, buf[:, tile(n)])
        v = yfn2[3 + n]
        for buf, f in ((iw14, v), (it14, roll(v, -32))):
            buf[:, tile(5 + n)] = f if n > 0 else jnp.where(low, buf[:, tile(5 + n)], f)

    def y_faces(n, _):
        at = pl.ds(pl.multiple_of(8 * n, 8), 8)
        value, parts = weno_parts(c18[at, :], v14[at, :], 64, lambda f: f[:, 128:1024])
        wy[at, :] = value
        for o in range(6):
            ay[o, at, :] = parts[o]
        return 0

    lax.fori_loop(0, nz // 8, y_faces, 0)

    @pl.when(owner)
    def _():
        pltpu.make_async_copy(r3, r3, p_recv.at[2]).wait()
        left = lax.broadcasted_iota(jnp.int32, (ns, 128), 1) < 64
        cols = []
        for i in range(7):
            one = r3[pl.ds(2 * i, ns, stride=16), :]
            two = r3[pl.ds(2 * i + 1, ns, stride=16), :]
            cols.append(
                jnp.concatenate(
                    [
                        jnp.where(left, one, roll(two, 64)),
                        jnp.where(left, roll(one, 64), two),
                    ],
                    0,
                )
            )
        y = dot(ring_t[...], jnp.concatenate(cols, 1))
        at = lax.broadcasted_iota(jnp.int32, (nt, 128), 1) & 31
        edge = jnp.zeros((nt, 128), F32)
        before, after = roll(y, 1, 0), roll(y, -1, 0)
        for i in range(7):
            s4[pl.ds(i, nt, stride=8), :] = y[:, tile(i)]
            if 1 <= i <= 5:
                k = 3 * (i - 1)
                edge = jnp.where((at >= k) & (at < k + 3), roll(before[:, tile(i)], k - 29), edge)
                edge = jnp.where((at >= 16 + k) & (at < 19 + k), roll(after[:, tile(i)], 16 + k), edge)
        s4[pl.ds(7, nt, stride=8), :] = edge

        def send4(i, _):
            g = lax.rem(t + i, nt)
            remote(s4.at[rows(g, 8)], r4.at[rows(t, 8)], s, g, p_send.at[3], p_recv.at[3]).start()
            return 0

        lax.fori_loop(1, nt, send4, 0)
        pltpu.make_async_copy(s4.at[rows(t, 8)], r4.at[rows(t, 8)], p_recv.at[3]).start()

    c10, w = c18[:, 256:896], w10[...]
    ch[0] = jnp.where(level == nz - 1, 0.0, 0.5 * (c10 + roll(c10, -1, 0)))
    ch[1] = jnp.where(level == nz - 1, 0.0, 0.5 * w)

    pltpu.make_async_copy(r4, r4, p_recv.at[3]).wait()
    cols = []
    for i in range(8):
        one = r4[pl.ds(i, ng, stride=8), :]
        modal[i, pl.ds(0, ng, stride=2), :] = roll(one, 8)
        modal[i, pl.ds(1, ng, stride=2), :] = roll(one, -24)
        cols.append(modal[i])
    p = dot_tn(minv[...], jnp.concatenate(cols, 1))
    edge = p[:, tile(7)]
    for i in range(7):
        v = p[:, tile(i)]
        if 1 <= i <= 5:
            k = 3 * (i - 1)
            v = jnp.where((slot >= 5) & (slot < 8), roll(edge, -3 - k), v)
            v = jnp.where((slot >= 40) & (slot < 43), roll(edge, 16 - k), v)
        p_buf[:, tile(i)] = v
    p = p_buf[...]
    upper = jnp.where(lax.broadcasted_iota(jnp.int32, p.shape, 0) == nz - 1, 0.0, roll(p, -1, 0))
    mid = iw14[...] - (upper - p)
    mw_buf[...] = mid[:, 128:768]
    d = dot_tn(dinv[...], it14[...] + GRAV * DT * mid)
    d_buf[...] = d
    d10 = d[:, 128:768]
    gz = roll(d10, -1, 0) - d10
    wz = ch[1] * gz
    oc[...] = d10 + DT * (wz + roll(wz, 1, 0))
    mw = mw_buf[...]
    ow[...] = mw + DT * NU * spread(mw) + DT * (ch[0] * gz)

    def last(n, _):
        at = pl.ds(pl.multiple_of(8 * n, 8), 8)
        p14, d14 = p_buf[at, :], d_buf[at, :]
        p10, dx = p14[:, 128:768], d14[:, 128:768]
        mu = iu10[at, :] - (roll(p10, -1) - p10)
        mv = iv10[at, :] - (roll(p14, -64)[:, 128:768] - p10)
        gx = roll(dx, -1) - dx
        gy = roll(d14, -64) - d14
        total = KAPPA * spread(dx)
        ty = jnp.zeros_like(d14)
        for o in range(6):
            total = total + roll(ax[o, at, :] * gx, o - 2)
            ty = ty + roll(ay[o, at, :] * gy, 64 * (o - 2))
        ou[at, :] = mu + DT * NU * spread(mu) + DT * (wx[at, :] * gx)
        ov[at, :] = mv + DT * NU * spread(mv) + DT * (wy[at, :] * gy)[:, 128:768]
        oc[at, :] = oc[at, :] + DT * (total + ty[:, 128:768])
        return 0

    lax.fori_loop(0, nz // 8, last, 0)

    for src, dst in ((ou, out_u), (ov, out_v), (ow, out_w), (oc, out_c)):
        for r in range(ROWS):
            v = roll(src[:, tile((r + 1) // 2)], -8 - 64 * ((r + 1) % 2))
            dst[pl.ds(r, nz, stride=ROWS), :] = v[:, :COLS]

    for copy in first_halo + second_halo:
        copy.wait_send()

    @pl.when(owner)
    def _():
        for n, buf, count in ((0, s1, ng - 1), (1, s2, 8 * (ns - 1)), (2, s3, 16 * (ns - 1)), (3, s4, 8 * (nt - 1))):
            part = buf.at[pl.ds(0, count)]
            pltpu.make_async_copy(part, part, p_send.at[n]).wait()

    @pl.when(t >= ng)
    def _():
        pltpu.make_async_copy(s1, s1, p_send.at[0]).wait()
        loads[8].wait()


def call(ns, nt, nz, consts, *args):
    ng = nz // 2
    vmem, anywhere = pl.BlockSpec(memory_space=pltpu.VMEM), pl.BlockSpec(memory_space=pl.ANY)
    smem = pl.BlockSpec(memory_space=pltpu.SMEM)

    def buf(*shape):
        return pltpu.VMEM(shape, F32)

    out = jax.ShapeDtypeStruct((nz * ROWS, COLS), F32)
    return pl.pallas_call(
        functools.partial(kernel, ns, nt, nz),
        out_shape=[out] * 4,
        in_specs=[anywhere] * 8 + [vmem] * 3 + [smem] + [vmem] * 4 + [anywhere, vmem],
        out_specs=[vmem] * 4,
        scratch_shapes=[
            buf(8, nz * ROWS, COLS), buf(136, 128),
            buf(nz, 640), buf(nz, 896), buf(nz, 640), buf(nz, 1152),
            buf(nz, 640), buf(nz, 640), buf(nz, 896), buf(nz, 896), buf(8, nz, 128),
            buf(2, nz, 128), buf(2, nz, 128), buf(2, nz, 128), buf(2, nz, 128),
            buf(nz, 128), buf(nz, 128), buf(nz, 128), buf(nz, 128),
            buf(5, nz, 128), buf(5, nz, 128), buf(5, nz, 128), buf(5, nz, 128),
            buf(ng, 4, 128), buf(nt, 4, 128), buf(8 * ns, 128), buf(8 * ns, 128),
            buf(16 * ns, 128), buf(16 * ns, 128), buf(8 * nt, 128), buf(8 * ng, 128),
            buf(6, nz, 640), buf(nz, 640), buf(6, nz, 896), buf(nz, 896), buf(2, nz, 640),
            buf(nz, 896), buf(nz, 896), buf(nz, 640),
            buf(nz, 640), buf(nz, 640), buf(nz, 640), buf(nz, 640),
            pltpu.SemaphoreType.DMA((9,)), pltpu.SemaphoreType.DMA((8,)), pltpu.SemaphoreType.DMA((8,)),
            pltpu.SemaphoreType.DMA((4,)), pltpu.SemaphoreType.DMA((4,)),
        ],
        compiler_params=pltpu.CompilerParams(
            collective_id=0, has_side_effects=True, vmem_limit_bytes=40 * 1024 * 1024
        ),
    )(*args, *consts)


def solution(mesh):
    ns, nt = mesh.shape["ys"], mesh.shape["xs"]
    consts = tables(ns, nt)

    def shards(*args):
        nz = args[0].shape[0]
        flat = [v.reshape(nz * ROWS, COLS) for v in args[:8]]
        out = call(ns, nt, nz, [jnp.asarray(v) for v in consts], *flat, *args[8:])
        return tuple(v.reshape(nz, ROWS, COLS) for v in out)

    block = P(None, "ys", "xs")
    return jax.shard_map(
        shards, mesh=mesh, in_specs=(block,) * 8 + (P(),) * 4, out_specs=(block,) * 4, check_vma=False
    )
```

profile of v0, /device:TPU:1, one launch (start us, length us, event | category | flops | bytes accessed | tf_op | source)
XLA Modules:
  0.0 71.4 jit_solution(13716316041340021421)
XLA Ops:
  0.6 0.0 copy-start.13
  0.6 0.0 copy-start.12
  0.7 0.0 copy-start.11
  0.7 0.0 copy-start.10
  0.7 1.1 %copy.22 = f32[48,8,32]{2,1,0:T(8,128)S(1)} copy(f32[48,8,32]{0,2,1:T(8,128)} %param.18) | data formatting | bytes 98304 | tf_op args[0]
  1.8 0.0 copy-start
  1.8 0.0 copy-start.2
  1.8 0.0 copy-start.7
  1.8 1.1 %copy.23 = f32[48,8,32]{2,1,0:T(8,128)S(1)} copy(f32[48,8,32]{0,2,1:T(8,128)} %param.19) | data formatting | bytes 98304 | tf_op args[1]
  2.9 1.0 %copy.24 = f32[48,8,32]{2,1,0:T(8,128)S(1)} copy(f32[48,8,32]{0,2,1:T(8,128)} %param.20) | data formatting | bytes 98304 | tf_op args[2]
  4.0 1.0 %copy.25 = f32[48,8,32]{2,1,0:T(8,128)S(1)} copy(f32[48,8,32]{0,2,1:T(8,128)} %param.21) | data formatting | bytes 98304 | tf_op args[3]
  5.0 0.0 copy-done.10
  5.0 0.1 copy.26
  5.2 0.0 copy-done.11
  5.2 0.1 copy.27
  5.3 0.0 copy-done.12
  5.3 0.1 copy.28
  5.5 0.0 copy-done.13
  5.5 0.1 copy.29
  5.6 0.0 copy-done
  5.6 0.0 copy-done.2
  5.6 0.0 copy-done.7
  5.6 0.0 copy-start.1
  5.6 0.9 %copy-done.1 = f32[256,128]{1,0:T(8,128)S(1)} copy-done((f32[256,128]{1,0:T(8,128)S(1)}, f32[256,128]{1,0:T(8,128)}, u32[]{:S(2)}) %copy-start.1) | copy-done | bytes 131096
  6.5 0.0 copy-start.3
  6.5 0.8 %copy-done.3 = f32[128,128]{1,0:T(8,128)S(1)} copy-done((f32[128,128]{1,0:T(8,128)S(1)}, f32[128,128]{1,0:T(8,128)}, u32[]{:S(2)}) %copy-start.3) | copy-done | bytes 65560
  7.4 0.0 copy-start.4
  7.4 0.7 %copy-done.4 = f32[48,48]{1,0:T(8,128)S(1)} copy-done((f32[48,48]{1,0:T(8,128)S(1)}, f32[48,48]{1,0:T(8,128)}, u32[]{:S(2)}) %copy-start.4) | copy-done | bytes 9240
  8.1 0.0 copy-start.5
  8.1 0.7 %copy-done.5 = f32[48,48]{1,0:T(8,128)S(1)} copy-done((f32[48,48]{1,0:T(8,128)S(1)}, f32[48,48]{1,0:T(8,128)}, u32[]{:S(2)}) %copy-start.5) | copy-done | bytes 9240
  8.9 0.0 copy-start.6
  8.9 0.7 %copy-done.6 = f32[48,48]{1,0:T(8,128)S(1)} copy-done((f32[48,48]{1,0:T(8,128)S(1)}, f32[48,48]{1,0:T(8,128)}, u32[]{:S(2)}) %copy-start.6) | copy-done | bytes 9240
  9.6 0.0 copy-start.8
  9.6 0.7 %copy-done.8 = f32[32,32]{1,0:T(8,128)S(1)} copy-done((f32[32,32]{1,0:T(8,128)S(1)}, f32[32,32]{1,0:T(8,128)}, u32[]{:S(2)}) %copy-start.8) | copy-done | bytes 4120
  10.3 0.0 copy-start.9
  10.3 0.7 copy-done.9
  11.0 57.3 %shard_map.201 = (f32[384,32]{1,0:T(8,128)S(1)}, f32[384,32]{1,0:T(8,128)S(1)}, f32[384,32]{1,0:T(8,128)S(1)}, f32[384,32]{1,0:T(8,128)S(1)}) custom-call(f32[384,32]{1,0:T(8,128)S(1)} %bitcast.12, f32[384,32]{1,0:T(8,128)S(1)} %bitcast.13, f32[384,32]{1,0:T(8,128)S(1)} %bitcast.14, f32[384,32]{1,0:T(8,128)S(1)} %bitcast.15, f32[384,32]{1,0:T(8,128)S(1)} %bitcast.16, ...), custom_call_target="tpu_custom_call" | custom-call | tf_op jit(solution)/shard_map/pallas_call | solution.py:528
  68.3 0.8 %copy.30 = f32[48,8,32]{0,2,1:T(8,128)} copy(f32[48,8,32]{2,1,0:T(8,128)S(1)} %bitcast.23) | data formatting | bytes 98304
  69.0 0.8 %copy.31 = f32[48,8,32]{0,2,1:T(8,128)} copy(f32[48,8,32]{2,1,0:T(8,128)S(1)} %bitcast.22) | data formatting | bytes 98304
  69.8 0.8 %copy.32 = f32[48,8,32]{0,2,1:T(8,128)} copy(f32[48,8,32]{2,1,0:T(8,128)S(1)} %bitcast.21) | data formatting | bytes 98304
  70.6 0.8 %copy.33 = f32[48,8,32]{0,2,1:T(8,128)} copy(f32[48,8,32]{2,1,0:T(8,128)S(1)} %bitcast.20) | data formatting | bytes 98304
Async XLA Ops:
  0.6 4.8 %copy-start.13 = (f32[48,8,32]{0,2,1:T(8,128)S(1)}, f32[48,8,32]{0,2,1:T(8,128)}, u32[]{:S(2)}) copy-start(f32[48,8,32]{0,2,1:T(8,128)} %param.25) | copy-start | bytes 147460
  0.6 4.7 %copy-start.12 = (f32[48,8,32]{0,2,1:T(8,128)S(1)}, f32[48,8,32]{0,2,1:T(8,128)}, u32[]{:S(2)}) copy-start(f32[48,8,32]{0,2,1:T(8,128)} %param.24) | copy-start | bytes 147460
  0.7 4.5 %copy-start.11 = (f32[48,8,32]{0,2,1:T(8,128)S(1)}, f32[48,8,32]{0,2,1:T(8,128)}, u32[]{:S(2)}) copy-start(f32[48,8,32]{0,2,1:T(8,128)} %param.23) | copy-start | bytes 147460
  0.7 4.4 %copy-start.10 = (f32[48,8,32]{0,2,1:T(8,128)S(1)}, f32[48,8,32]{0,2,1:T(8,128)}, u32[]{:S(2)}) copy-start(f32[48,8,32]{0,2,1:T(8,128)} %param.22) | copy-start | bytes 147460
  1.8 3.8 %copy-start = (f32[16,136,128]{2,1,0:T(8,128)S(1)}, f32[16,136,128]{2,1,0:T(8,128)}, u32[]{:S(2)}) copy-start(f32[16,136,128]{2,1,0:T(8,128)} %constant.16.clone.spec_h) | copy-start | bytes 3342340
  1.8 3.8 %copy-start.2 = (f32[128,128]{1,0:T(8,128)S(1)}, f32[128,128]{1,0:T(8,128)}, u32[]{:S(2)}) copy-start(f32[128,128]{1,0:T(8,128)} %constant.17.clone.lamy) | copy-start | bytes 196612
  1.8 3.8 %copy-start.7 = (f32[32,32]{1,0:T(8,128)S(1)}, f32[32,32]{1,0:T(8,128)}, u32[]{:S(2)}) copy-start(f32[32,32]{1,0:T(8,128)} %constant.13.clone.ring_t) | copy-start | bytes 12292
  5.6 0.9 %copy-start.1 = (f32[256,128]{1,0:T(8,128)S(1)}, f32[256,128]{1,0:T(8,128)}, u32[]{:S(2)}) copy-start(f32[256,128]{1,0:T(8,128)} %constant.15.clone.yinv) | copy-start | bytes 393220
  6.5 0.8 %copy-start.3 = (f32[128,128]{1,0:T(8,128)S(1)}, f32[128,128]{1,0:T(8,128)}, u32[]{:S(2)}) copy-start(f32[128,128]{1,0:T(8,128)} %constant.14.clone.yfwd) | copy-start | bytes 196612
  7.4 0.7 %copy-start.4 = (f32[48,48]{1,0:T(8,128)S(1)}, f32[48,48]{1,0:T(8,128)}, u32[]{:S(2)}) copy-start(f32[48,48]{1,0:T(8,128)} %dinv.1) | copy-start | bytes 27652
  8.1 0.7 %copy-start.5 = (f32[48,48]{1,0:T(8,128)S(1)}, f32[48,48]{1,0:T(8,128)}, u32[]{:S(2)}) copy-start(f32[48,48]{1,0:T(8,128)} %vecs.1) | copy-start | bytes 27652
  8.9 0.7 %copy-start.6 = (f32[48,48]{1,0:T(8,128)S(1)}, f32[48,48]{1,0:T(8,128)}, u32[]{:S(2)}) copy-start(f32[48,48]{1,0:T(8,128)} %minv.1) | copy-start | bytes 27652
  9.6 0.7 %copy-start.8 = (f32[32,32]{1,0:T(8,128)S(1)}, f32[32,32]{1,0:T(8,128)}, u32[]{:S(2)}) copy-start(f32[32,32]{1,0:T(8,128)} %constant.12.clone.ring) | copy-start | bytes 12292
  10.3 0.7 copy-start.9
where the time goes:
time: 71.9 us; the launch traced here: 71.4 us
  Pallas kernels  57.3 us (80%)
  local copies, waits for them, and re-layouts  13.3 us (18%)
  between operations  0.83 us (1%)
    pallas_call x1, Pallas kernels, call(): pl.pallas_call(functools.partial(kernel, ns, nt, nz), out_shape=[out] * 4...  57.3 us
    unnamed x40, local copies, waits for them, and re-layouts  13.3 us

commit v1 on v0

--- a/solution.py
+++ b/solution.py
@@ -64,15 +64,43 @@
             ylam.append(4 * np.sin(np.pi * k / ny) ** 2)
     ybase = np.stack(ybase)
     lamy = np.broadcast_to(np.array(ylam)[:, None], (ny, 128))
-    yfwd = ybase.reshape(ny, ns, 4, 2).transpose(0, 3, 2, 1).reshape(ny, ny)
+    yfwd = ybase.reshape(ny, ns, 2, 4).transpose(0, 3, 2, 1).reshape(ny, ny)
     yinv = np.zeros((ns, 16, ny))
     for s in range(ns):
         for r in range(14):
             yinv[s, r] = ybase[:, (ROWS * s - 3 + r) % ny]
-    yinv = yinv.reshape(16 * ns, ny)
+    after = ybase[:, (ROWS * np.arange(ns) + ROWS) % ny]
     ring = ring.reshape(nt, nt)
-    out = (ring, ring.T, yfwd, yinv, spectral, lamy)
-    return tuple(np.ascontiguousarray(v).astype(np.float32) for v in out)
+    parts = (lamy, yinv.reshape(16 * ns, ny), yfwd, after, ring, np.roll(ring, -1, 1), ring.T)
+    packed = np.zeros((sum(len(v) for v in parts), 128))
+    at, places = 0, []
+    for v in parts:
+        packed[at : at + len(v), : v.shape[1]] = v
+        places.append((at, at + len(v), v.shape[1]))
+        at += len(v)
+    return packed.astype(np.float32), np.ascontiguousarray(spectral).astype(np.float32), tuple(places)
+
+
+def owners(nt, ng):
+    if (nt, ng) != (32, 24):
+        return (lambda n: n), (lambda t: t), (lambda t: t < ng)
+
+    def index_of(n):
+        h = n // 2
+        late = h // 8
+        y = h - 8 * late
+        y = y + late * 4 * (y // 2)
+        return 4 * y + 2 * late + n % 2
+
+    def pair_of(t):
+        y, late = t // 4, (t // 2) % 2
+        return 2 * (y - late * 4 * (y // 4)) + 16 * late + t % 2
+
+    def has(t):
+        y, late = t // 4, (t // 2) % 2
+        return (late == 0) | ((y + 2) % 8 < 4)
+
+    return index_of, pair_of, has
 
 
 def dot(a, b):
@@ -142,38 +170,64 @@
 
 
 def kernel(
-    ns, nt, nz,
-    fu_h, fv_h, fw_h, fc_h, iu_h, iv_h, iw_h, it_h, dinv, vecs, minv, eig, ring, ring_t, yfwd, yinv, spec_h, lamy,
+    ns, nt, nz, places,
+    fu_h, fv_h, fw_h, fc_h, iu_h, iv_h, iw_h, it_h, dinv_h, vecs_h, minv_h, eig, packed_h, spec_h,
     out_u, out_v, out_w, out_c,
-    raw, spec, u10, v14, w10, c18, iu10, iv10, iw14, it14, modal,
-    xe, xw, xfw, xfe, yn1, ys1, yfs1, yfn1, yn2, ys2, yfs2, yfn2,
+    raw, mats, packed, spec, rhs, u10, v14, w10, c18, iu10, iv10, iw14, it14, modal,
+    xe, xw, xfw, xfe, yn2, ys2, yfs2, yfn2,
     s1, r1, s2, r2, s3, r3, s4, r4,
     ax, wx, ay, wy, ch, d_buf, p_buf, mw_buf, ou, ov, ow, oc,
-    in_sem, h_send, h_recv, p_send, p_recv,
+    in_sem, h_send, h_recv, p_send, p_recv, ready,
 ):
     ng = nz // 2
     s, t = lax.axis_index("ys"), lax.axis_index("xs")
-    owner = t < ng
+    index_of, pair_of, has = owners(nt, ng)
+    owner = has(t)
+    other = jnp.logical_not(owner)
+    mine = pair_of(t)
+    late = nt - ng
+
+    barrier = pltpu.get_barrier_semaphore()
+
+    def greet(a, b):
+        pl.semaphore_signal(barrier, 1, device_id=(a, b), device_id_type=MESH)
+
+    def greet_x(i, _):
+        greet(s, lax.rem(t + i, nt))
+        return 0
+
+    def greet_y(i, _):
+        greet(lax.rem(s + i, ns), t)
+        return 0
+
+    east, west = lax.rem(t + 1, nt), lax.rem(t + nt - 1, nt)
+    north, south = lax.rem(s + 1, ns), lax.rem(s + ns - 1, ns)
+    twin = t + 1 - 2 * lax.rem(t, 2)
+
+    @pl.when(owner)
+    def _():
+        lax.fori_loop(1, nt, greet_x, 0)
+        lax.fori_loop(1, ns, greet_y, 0)
+
+    if late:
+
+        @pl.when(other)
+        def _():
+            greet(north, t)
+            greet(south, t)
+            greet(s, twin)
 
     loads = []
     for n, src in enumerate((iu_h, iv_h, iw_h, it_h, fc_h, fu_h, fv_h, fw_h)):
-        loads.append(pltpu.make_async_copy(src, raw.at[n], in_sem.at[n]))
+        dst = raw.at[n, pl.ds(1, ROWS), pl.ds(8, COLS)]
+        loads.append(pltpu.make_async_copy(src, dst, in_sem.at[n]))
     loads.append(pltpu.make_async_copy(spec_h.at[s], spec, in_sem.at[8]))
-    for copy in loads:
-        copy.start()
-
-    barrier = pltpu.get_barrier_semaphore()
-
-    def greet_x(i, _):
-        pl.semaphore_signal(barrier, 1, device_id=(s, lax.rem(t + i, nt)), device_id_type=MESH)
-        return 0
-
-    def greet_y(i, _):
-        pl.semaphore_signal(barrier, 1, device_id=(lax.rem(s + i, ns), t), device_id_type=MESH)
-        return 0
-
-    lax.fori_loop(1, nt, greet_x, 0)
-    lax.fori_loop(1, ns, greet_y, 0)
+    loads.append(pltpu.make_async_copy(packed_h, packed, in_sem.at[9]))
+    for n, src in enumerate((vecs_h, minv_h, dinv_h)):
+        loads.append(pltpu.make_async_copy(src, mats.at[n], in_sem.at[10 + n]))
+    order = (0, 1, 2, 10, 9, 8, 3, 4, 5, 6, 7, 11, 12)
+    for n in order:
+        loads[n].start()
 
     lane = lax.broadcasted_iota(jnp.int32, (nz, 128), 1)
     slot = lane & 63
@@ -188,11 +242,14 @@
     def tile(n):
         return slice(128 * n, 128 * n + 128)
 
+    def table(n):
+        first, end, width = places[n]
+        return packed[first:end, :width]
+
     def place(n, buf, first):
-        loads[n].wait()
-        for r in range(ROWS):
-            at = 128 * first + 64 * (r + 1) + 8
-            buf[:, at : at + COLS] = raw[n, pl.ds(r, nz, stride=ROWS), :]
+        for k in range(5):
+            v = raw[n, 2 * k : 2 * k + 2].reshape(128, nz)
+            buf[:, tile(first + k)] = v.T
 
     def pack_x(fields, out):
         total = jnp.zeros((nz, 128), F32)
@@ -229,112 +286,174 @@
             src_ref=src, dst_ref=dst, send_sem=send, recv_sem=recv, device_id=(ds, dt), device_id_type=MESH
         )
 
-    east, west = lax.rem(t + 1, nt), lax.rem(t + nt - 1, nt)
-    north, south = lax.rem(s + 1, ns), lax.rem(s + ns - 1, ns)
-
+    loads[0].wait()
+    loads[1].wait()
+    loads[2].wait()
+    iu = raw[0, 1:9, 8:40].reshape(ROWS * COLS, nz)
+    iv = raw[1, 1:9, 8:40].reshape(ROWS * COLS, nz)
+    iw = raw[2, 1:9, 8:40].reshape(ROWS * COLS, nz)
+    first_col = lax.broadcasted_iota(jnp.int32, iu.shape, 0) % COLS == 0
+    before = jnp.where(first_col, 0.0, roll(iu, 1, 0))
+    behind = jnp.concatenate([jnp.zeros((COLS, nz), F32), iv[: 7 * COLS]], 0)
+    rhs[0:256, :] = (iu - before) + (iv - behind)
+    rhs[256:288, :] = -iv[7 * COLS :]
+    rhs[288:416, :] = jnp.zeros((128, nz), F32)
+    for r in range(ROWS):
+        at = 288 + 32 * (r % 4) + r // 4
+        rhs[at : at + 1, :] = -raw[0, r + 1, 39:40, :]
+    loads[10].wait()
+    vt = mats[0].T
+    next_vt = jnp.concatenate([vt[:, 1:], jnp.zeros((nz, 1), F32)], 1)
+    main = dot_nt(vt, rhs[0:256, :]) + dot_nt(vt - next_vt, iw)
+    extra = dot_nt(vt, rhs[256:416, :])
+    modal[0] = main[:, :128]
+    modal[1] = main[:, 128:]
+    modal[2] = jnp.concatenate([extra[:, :32], jnp.zeros((nz, 96), F32)], 1)
+    modal[3] = extra[:, 32:]
+    for i in range(4):
+        even = modal[i, pl.ds(0, ng, stride=2), :]
+        odd = modal[i, pl.ds(1, ng, stride=2), :]
+        if i < 2:
+            s1[pl.ds(i, ng, stride=8), :] = even
+            s1[pl.ds(2 + i, ng, stride=8), :] = odd
+        elif i == 2:
+            s1[pl.ds(4, ng, stride=8), :] = jnp.where(lane_g < 32, even, roll(odd, 32))
+        else:
+            s1[pl.ds(5, ng, stride=8), :] = jnp.where((lane_g & 31) < 2, even, roll(odd, 2))
+            s1[pl.ds(6, ng, stride=8), :] = jnp.zeros((ng, 128), F32)
+            s1[pl.ds(7, ng, stride=8), :] = jnp.zeros((ng, 128), F32)
+
+    @pl.when(owner)
+    def _():
+        pl.semaphore_wait(barrier, ng - 1 + ns - 1)
+
+    if late:
+
+        @pl.when(other)
+        def _():
+            pl.semaphore_wait(barrier, ng + 3)
+
+    def send1(i, _):
+        g = lax.rem(t + i, ng)
+        to = index_of(g)
+
+        @pl.when(to != t)
+        def _():
+            remote(s1.at[rows(g, 8)], r1.at[rows(t, 8)], s, to, p_send.at[0], p_recv.at[0]).start()
+
+        return 0
+
+    lax.fori_loop(0, ng, send1, 0)
+
+    @pl.when(owner)
+    def _():
+        pltpu.make_async_copy(s1.at[rows(mine, 8)], r1.at[rows(t, 8)], p_recv.at[0]).start()
+
+    if late:
+
+        @pl.when(other)
+        def _():
+            def report(i, _):
+                g = index_of(i)
+                pl.semaphore_signal(ready, 1, device_id=(s, g), device_id_type=MESH)
+                return 0
+
+            lax.fori_loop(0, ng, report, 0)
+
+    for n, buf, first in ((3, it14, 1), (4, c18, 2), (5, u10, 0), (6, v14, 1), (7, w10, 0)):
+        loads[n].wait()
+        place(n, buf, first)
     place(0, iu10, 0)
     place(1, iv10, 0)
-    pack_x(((iu10, 0, 31, 6, 1), (iv10, 0, 31, 7, 1)), xe.at[0])
-    pack_x(((iu10, 0, 0, 6, 1), (iv10, 0, 0, 7, 1)), xw.at[0])
-    yn1[...] = pair(iu10[:, tile(4)], iv10[:, tile(4)])
-    ys1[...] = pair(iu10[:, tile(0)], iv10[:, tile(0)])
-
-    pl.semaphore_wait(barrier, nt - 1 + ns - 1)
-    first_halo = [
-        remote(xe.at[0], xfw.at[0], s, east, h_send.at[0], h_recv.at[0]),
-        remote(yn1, yfs1, north, t, h_send.at[1], h_recv.at[1]),
-        remote(xw.at[0], xfe.at[0], s, west, h_send.at[2], h_recv.at[2]),
-        remote(ys1, yfn1, south, t, h_send.at[3], h_recv.at[3]),
-    ]
-    for copy in first_halo:
-        copy.start()
-
     place(2, iw14, 1)
-    place(3, it14, 1)
-    place(4, c18, 2)
-    place(5, u10, 0)
-    place(6, v14, 1)
-    place(7, w10, 0)
-
-    pack_x(((iw14, 1, 29, 0, 3), (it14, 1, 29, 3, 3), (u10, 0, 29, 8, 3), (c18, 2, 27, 11, 5)), xe.at[1])
-    pack_x(((iw14, 1, 0, 0, 3), (it14, 1, 0, 3, 3), (u10, 0, 0, 8, 2), (c18, 2, 0, 11, 5)), xw.at[1])
+
+    pack_x(((iw14, 1, 29, 0, 3), (it14, 1, 29, 3, 3), (iu10, 0, 31, 6, 1), (iv10, 0, 31, 7, 1), (u10, 0, 29, 8, 3), (c18, 2, 27, 11, 5)), xe)
+    pack_x(((iw14, 1, 0, 0, 3), (it14, 1, 0, 3, 3), (iu10, 0, 0, 6, 1), (iv10, 0, 0, 7, 1), (u10, 0, 0, 8, 2), (c18, 2, 0, 11, 5)), xw)
     for n in range(3):
         yn2[n] = pair(c18[:, tile(4 + n)], v14[:, tile(3 + n)])
         ys2[n] = pair(c18[:, tile(2 + n)], v14[:, tile(1 + n)])
     for n in range(2):
         yn2[3 + n] = pair(iw14[:, tile(4 + n)], it14[:, tile(4 + n)])
         ys2[3 + n] = pair(iw14[:, tile(1 + n)], it14[:, tile(1 + n)])
-
-    first_halo[0].wait_recv()
-    unpack_x(xfw.at[0], ((iu10, 0, -1, 6, 1), (iv10, 0, -1, 7, 1)))
-    first_halo[1].wait_recv()
-    v = yfs1[...]
-    iu10[:, tile(0)] = jnp.where(low, v, iu10[:, tile(0)])
-    iv10[:, tile(0)] = jnp.where(low, roll(v, -32), iv10[:, tile(0)])
-
-    iu, iv, iw = iu10[...], iv10[...], iw14[:, 128:768]
-    below = jnp.where(level == 0, 0.0, roll(iw, 1, 0))
-    div = iu - roll(iu, 1) + (iv - roll(iv, 64)) + (iw - below)
-    div = roll(div, -64)[:, :512]
-    div = dot_tn(vecs[...], div)
-    half = (lane_g & 63) < 32
-    for i in range(4):
-        modal[i] = div[:, tile(i)]
-        even = modal[i, pl.ds(0, ng, stride=2), :]
-        odd = modal[i, pl.ds(1, ng, stride=2), :]
-        s1[:, i, :] = jnp.where(half, roll(even, -8), roll(odd, 24))
-
-    def send1(i, _):
-        g = lax.rem(t + i, ng)
-
-        @pl.when(g != t)
-        def _():
-            remote(s1.at[g], r1.at[t], s, g, p_send.at[0], p_recv.at[0]).start()
-
-        return 0
-
-    lax.fori_loop(0, ng, send1, 0)
-
-    @pl.when(owner)
-    def _():
-        pltpu.make_async_copy(s1.at[t], r1.at[t], p_recv.at[0]).start()
-
-    second_halo = [
-        remote(xe.at[1], xfw.at[1], s, east, h_send.at[4], h_recv.at[4]),
-        remote(yn2, yfs2, north, t, h_send.at[5], h_recv.at[5]),
-        remote(xw.at[1], xfe.at[1], s, west, h_send.at[6], h_recv.at[6]),
-        remote(ys2, yfn2, south, t, h_send.at[7], h_recv.at[7]),
-    ]
-    for copy in second_halo:
-        copy.start()
+    yn2[5] = pair(iu10[:, tile(4)], iv10[:, tile(4)])
+    ys2[5] = pair(iu10[:, tile(0)], iv10[:, tile(0)])
+    loads[9].wait()
 
     @pl.when(owner)
     def _():
         pltpu.make_async_copy(r1, r1, p_recv.at[0]).wait()
-        x = jnp.concatenate([r1[:, i, :] for i in range(4)], 1)
-        y = dot(ring[...], x)
+        x = jnp.concatenate([r1[pl.ds(i, nt, stride=8), :] for i in range(5)], 1)
+        y = dot(table(4), x)
+        z = dot(table(5), r1[pl.ds(5, nt, stride=8), :])
+        first = (lax.broadcasted_iota(jnp.int32, (nt, 128), 1) & 31) == 0
+        at = lax.broadcasted_iota(jnp.int32, (ns, 128), 1)
+        parts = [y[:, tile(i)] + jnp.where(first, roll(z, -i), 0.0) for i in range(4)]
         for q in range(2):
             for i in range(4):
-                s2[pl.ds(4 * q + i, ns, stride=8), :] = y[q * ns : (q + 1) * ns, tile(i)]
+                s2[pl.ds(4 * q + i, ns, stride=16), :] = parts[i][q * ns : (q + 1) * ns]
+        s2[pl.ds(8, ns, stride=16), :] = jnp.where(at < 64, y[:ns, tile(4)], roll(y[ns:, tile(4)], 64))
+        for i in range(9, 16):
+            s2[pl.ds(i, ns, stride=16), :] = jnp.zeros((ns, 128), F32)
 
         def send2(i, _):
             j = lax.rem(s + i, ns)
-            remote(s2.at[rows(j, 8)], r2.at[rows(s, 8)], j, t, p_send.at[1], p_recv.at[1]).start()
+            remote(s2.at[rows(j, 16)], r2.at[rows(s, 16)], j, t, p_send.at[1], p_recv.at[1]).start()
             return 0
 
         lax.fori_loop(1, ns, send2, 0)
-        pltpu.make_async_copy(s2.at[rows(s, 8)], r2.at[rows(s, 8)], p_recv.at[1]).start()
-
-    first_halo[2].wait_recv()
-    unpack_x(xfe.at[0], ((iu10, 0, 32, 6, 1), (iv10, 0, 32, 7, 1)))
-    first_halo[3].wait_recv()
-    v = yfn1[...]
-    iu10[:, tile(4)] = jnp.where(low, iu10[:, tile(4)], v)
-    iv10[:, tile(4)] = jnp.where(low, iv10[:, tile(4)], roll(v, -32))
-    second_halo[0].wait_recv()
-    unpack_x(xfw.at[1], ((iw14, 1, -3, 0, 3), (it14, 1, -3, 3, 3), (u10, 0, -3, 8, 3), (c18, 2, -5, 11, 5)))
-    second_halo[2].wait_recv()
-    unpack_x(xfe.at[1], ((iw14, 1, 32, 0, 3), (it14, 1, 32, 3, 3), (u10, 0, 32, 8, 2), (c18, 2, 32, 11, 5)))
+        pltpu.make_async_copy(s2.at[rows(s, 16)], r2.at[rows(s, 16)], p_recv.at[1]).start()
+
+    if late:
+
+        @pl.when(owner)
+        def _():
+            pl.semaphore_wait(ready, late)
+
+    halos = [
+        remote(xe, xfw, s, east, h_send.at[0], h_recv.at[0]),
+        remote(yn2, yfs2, north, t, h_send.at[1], h_recv.at[1]),
+        remote(xw, xfe, s, west, h_send.at[2], h_recv.at[2]),
+        remote(ys2, yfn2, south, t, h_send.at[3], h_recv.at[3]),
+    ]
+    for copy in halos:
+        copy.start()
+
+    @pl.when(owner)
+    def _():
+        loads[8].wait()
+        pltpu.make_async_copy(r2, r2, p_recv.at[1]).wait()
+        part = [
+            jnp.concatenate([r2[pl.ds(2 * n + i, ns, stride=16), :] for i in range(2)], 0) for n in range(4)
+        ]
+        group = lax.broadcasted_iota(jnp.int32, (2 * ns, 128), 1) // 32
+        x = []
+        for r in range(4):
+            v = roll(part[0], -32 * r)
+            for n in range(1, 4):
+                v = jnp.where(group == n, roll(part[n], 32 * (n - r)), v)
+            x.append(v)
+        x = jnp.concatenate(x, 0)
+        y = dot(table(2), x) + dot(table(3), r2[pl.ds(8, ns, stride=16), :])
+        inner = spec[0:128, :]
+        y = dot(y, inner)
+        wide = lax.broadcasted_iota(jnp.int32, (1, 128), 1)
+        own = jnp.where((wide & 32) == 0, eig[2 * mine], eig[2 * mine + 1])
+        y = -y / (own + table(0) + spec[128:129, :])
+        y = dot(table(1), dot_nt(y, inner))
+        s3[...] = y
+
+        def send3(i, _):
+            j = lax.rem(s + i, ns)
+            remote(s3.at[rows(j, 16)], r3.at[rows(s, 16)], j, t, p_send.at[2], p_recv.at[2]).start()
+            return 0
+
+        lax.fori_loop(1, ns, send3, 0)
+        pltpu.make_async_copy(s3.at[rows(s, 16)], r3.at[rows(s, 16)], p_recv.at[2]).start()
+
+    halos[0].wait_recv()
+    unpack_x(xfw, ((iw14, 1, -3, 0, 3), (it14, 1, -3, 3, 3), (iu10, 0, -1, 6, 1), (iv10, 0, -1, 7, 1), (u10, 0, -3, 8, 3), (c18, 2, -5, 11, 5)))
+    halos[2].wait_recv()
+    unpack_x(xfe, ((iw14, 1, 32, 0, 3), (it14, 1, 32, 3, 3), (iu10, 0, 32, 6, 1), (iv10, 0, 32, 7, 1), (u10, 0, 32, 8, 2), (c18, 2, 32, 11, 5)))
 
     def x_faces(n, _):
         at = pl.ds(pl.multiple_of(8 * n, 8), 8)
@@ -346,39 +465,14 @@
 
     lax.fori_loop(0, nz // 8, x_faces, 0)
 
-    @pl.when(owner)
-    def _():
-        loads[8].wait()
-        pltpu.make_async_copy(r2, r2, p_recv.at[1]).wait()
-        part = [
-            jnp.concatenate([r2[pl.ds(4 * q + i, ns, stride=8), :] for i in range(4)], 0) for q in range(2)
-        ]
-        left = lax.broadcasted_iota(jnp.int32, (4 * ns, 128), 1) < 64
-        x = jnp.concatenate(
-            [
-                jnp.where(left, part[0], roll(part[1], 64)),
-                jnp.where(left, roll(part[0], 64), part[1]),
-            ],
-            0,
-        )
-        inner = spec[0:128, :]
-        y = dot(dot(yfwd[...], x), inner)
-        wide = lax.broadcasted_iota(jnp.int32, (1, 128), 1)
-        own = jnp.where((wide & 32) == 0, eig[2 * t], eig[2 * t + 1])
-        y = -y / (own + lamy[...] + spec[128:129, :])
-        y = dot(yinv[...], dot_nt(y, inner))
-        s3[...] = y
-
-        def send3(i, _):
-            j = lax.rem(s + i, ns)
-            remote(s3.at[rows(j, 16)], r3.at[rows(s, 16)], j, t, p_send.at[2], p_recv.at[2]).start()
-            return 0
-
-        lax.fori_loop(1, ns, send3, 0)
-        pltpu.make_async_copy(s3.at[rows(s, 16)], r3.at[rows(s, 16)], p_recv.at[2]).start()
-
-    second_halo[1].wait_recv()
-    second_halo[3].wait_recv()
+    halos[1].wait_recv()
+    halos[3].wait_recv()
+    v = yfs2[5]
+    iu10[:, tile(0)] = jnp.where(low, v, iu10[:, tile(0)])
+    iv10[:, tile(0)] = jnp.where(low, roll(v, -32), iv10[:, tile(0)])
+    v = yfn2[5]
+    iu10[:, tile(4)] = jnp.where(low, iu10[:, tile(4)], v)
+    iv10[:, tile(4)] = jnp.where(low, iv10[:, tile(4)], roll(v, -32))
     for n in range(3):
         v = yfs2[n]
         for buf, k, f in ((c18, n, v), (v14, n - 1, roll(v, -32))):
@@ -423,7 +517,7 @@
                     0,
                 )
             )
-        y = dot(ring_t[...], jnp.concatenate(cols, 1))
+        y = dot(table(6), jnp.concatenate(cols, 1))
         at = lax.broadcasted_iota(jnp.int32, (nt, 128), 1) & 31
         edge = jnp.zeros((nt, 128), F32)
         before, after = roll(y, 1, 0), roll(y, -1, 0)
@@ -437,16 +531,18 @@
 
         def send4(i, _):
             g = lax.rem(t + i, nt)
-            remote(s4.at[rows(g, 8)], r4.at[rows(t, 8)], s, g, p_send.at[3], p_recv.at[3]).start()
+            remote(s4.at[rows(g, 8)], r4.at[rows(mine, 8)], s, g, p_send.at[3], p_recv.at[3]).start()
             return 0
 
         lax.fori_loop(1, nt, send4, 0)
-        pltpu.make_async_copy(s4.at[rows(t, 8)], r4.at[rows(t, 8)], p_recv.at[3]).start()
+        pltpu.make_async_copy(s4.at[rows(t, 8)], r4.at[rows(mine, 8)], p_recv.at[3]).start()
 
     c10, w = c18[:, 256:896], w10[...]
     ch[0] = jnp.where(level == nz - 1, 0.0, 0.5 * (c10 + roll(c10, -1, 0)))
     ch[1] = jnp.where(level == nz - 1, 0.0, 0.5 * w)
 
+    loads[11].wait()
+    loads[12].wait()
     pltpu.make_async_copy(r4, r4, p_recv.at[3]).wait()
     cols = []
     for i in range(8):
@@ -454,7 +550,7 @@
         modal[i, pl.ds(0, ng, stride=2), :] = roll(one, 8)
         modal[i, pl.ds(1, ng, stride=2), :] = roll(one, -24)
         cols.append(modal[i])
-    p = dot_tn(minv[...], jnp.concatenate(cols, 1))
+    p = dot_tn(mats[1], jnp.concatenate(cols, 1))
     edge = p[:, tile(7)]
     for i in range(7):
         v = p[:, tile(i)]
@@ -467,7 +563,7 @@
     upper = jnp.where(lax.broadcasted_iota(jnp.int32, p.shape, 0) == nz - 1, 0.0, roll(p, -1, 0))
     mid = iw14[...] - (upper - p)
     mw_buf[...] = mid[:, 128:768]
-    d = dot_tn(dinv[...], it14[...] + GRAV * DT * mid)
+    d = dot_tn(mats[2], it14[...] + GRAV * DT * mid)
     d_buf[...] = d
     d10 = d[:, 128:768]
     gz = roll(d10, -1, 0) - d10
@@ -497,58 +593,63 @@
     lax.fori_loop(0, nz // 8, last, 0)
 
     for src, dst in ((ou, out_u), (ov, out_v), (ow, out_w), (oc, out_c)):
-        for r in range(ROWS):
-            v = roll(src[:, tile((r + 1) // 2)], -8 - 64 * ((r + 1) % 2))
-            dst[pl.ds(r, nz, stride=ROWS), :] = v[:, :COLS]
-
-    for copy in first_halo + second_halo:
+        for k in range(5):
+            v = src[:, tile(k)].T
+            if k > 0:
+                dst[2 * k - 1] = v[8:40]
+            if k < 4:
+                dst[2 * k] = v[72:104]
+
+    for copy in halos:
         copy.wait_send()
 
     @pl.when(owner)
     def _():
-        for n, buf, count in ((0, s1, ng - 1), (1, s2, 8 * (ns - 1)), (2, s3, 16 * (ns - 1)), (3, s4, 8 * (nt - 1))):
+        for n, buf, count in ((0, s1, 8 * (ng - 1)), (1, s2, 16 * (ns - 1)), (2, s3, 16 * (ns - 1)), (3, s4, 8 * (nt - 1))):
             part = buf.at[pl.ds(0, count)]
             pltpu.make_async_copy(part, part, p_send.at[n]).wait()
 
-    @pl.when(t >= ng)
-    def _():
-        pltpu.make_async_copy(s1, s1, p_send.at[0]).wait()
-        loads[8].wait()
+    if late:
+
+        @pl.when(other)
+        def _():
+            pltpu.make_async_copy(s1, s1, p_send.at[0]).wait()
+            loads[8].wait()
 
 
 def call(ns, nt, nz, consts, *args):
     ng = nz // 2
+    packed, spectral, places = consts
     vmem, anywhere = pl.BlockSpec(memory_space=pltpu.VMEM), pl.BlockSpec(memory_space=pl.ANY)
     smem = pl.BlockSpec(memory_space=pltpu.SMEM)
 
     def buf(*shape):
         return pltpu.VMEM(shape, F32)
 
-    out = jax.ShapeDtypeStruct((nz * ROWS, COLS), F32)
+    out = jax.ShapeDtypeStruct((ROWS, COLS, nz), F32)
     return pl.pallas_call(
-        functools.partial(kernel, ns, nt, nz),
+        functools.partial(kernel, ns, nt, nz, places),
         out_shape=[out] * 4,
-        in_specs=[anywhere] * 8 + [vmem] * 3 + [smem] + [vmem] * 4 + [anywhere, vmem],
+        in_specs=[anywhere] * 11 + [smem] + [anywhere] * 2,
         out_specs=[vmem] * 4,
         scratch_shapes=[
-            buf(8, nz * ROWS, COLS), buf(136, 128),
+            buf(8, 10, 64, nz), buf(3, nz, nz), buf(*packed.shape), buf(136, 128), buf(416, nz),
             buf(nz, 640), buf(nz, 896), buf(nz, 640), buf(nz, 1152),
             buf(nz, 640), buf(nz, 640), buf(nz, 896), buf(nz, 896), buf(8, nz, 128),
-            buf(2, nz, 128), buf(2, nz, 128), buf(2, nz, 128), buf(2, nz, 128),
             buf(nz, 128), buf(nz, 128), buf(nz, 128), buf(nz, 128),
-            buf(5, nz, 128), buf(5, nz, 128), buf(5, nz, 128), buf(5, nz, 128),
-            buf(ng, 4, 128), buf(nt, 4, 128), buf(8 * ns, 128), buf(8 * ns, 128),
+            buf(6, nz, 128), buf(6, nz, 128), buf(6, nz, 128), buf(6, nz, 128),
+            buf(8 * ng, 128), buf(8 * nt, 128), buf(16 * ns, 128), buf(16 * ns, 128),
             buf(16 * ns, 128), buf(16 * ns, 128), buf(8 * nt, 128), buf(8 * ng, 128),
             buf(6, nz, 640), buf(nz, 640), buf(6, nz, 896), buf(nz, 896), buf(2, nz, 640),
             buf(nz, 896), buf(nz, 896), buf(nz, 640),
             buf(nz, 640), buf(nz, 640), buf(nz, 640), buf(nz, 640),
-            pltpu.SemaphoreType.DMA((9,)), pltpu.SemaphoreType.DMA((8,)), pltpu.SemaphoreType.DMA((8,)),
-            pltpu.SemaphoreType.DMA((4,)), pltpu.SemaphoreType.DMA((4,)),
+            pltpu.SemaphoreType.DMA((13,)), pltpu.SemaphoreType.DMA((4,)), pltpu.SemaphoreType.DMA((4,)),
+            pltpu.SemaphoreType.DMA((4,)), pltpu.SemaphoreType.DMA((4,)), pltpu.SemaphoreType.REGULAR,
         ],
         compiler_params=pltpu.CompilerParams(
-            collective_id=0, has_side_effects=True, vmem_limit_bytes=40 * 1024 * 1024
+            collective_id=0, has_side_effects=True, vmem_limit_bytes=60 * 1024 * 1024
         ),
-    )(*args, *consts)
+    )(*args, jnp.asarray(packed), jnp.asarray(spectral))
 
 
 def solution(mesh):
@@ -556,10 +657,9 @@
     consts = tables(ns, nt)
 
     def shards(*args):
-        nz = args[0].shape[0]
-        flat = [v.reshape(nz * ROWS, COLS) for v in args[:8]]
-        out = call(ns, nt, nz, [jnp.asarray(v) for v in consts], *flat, *args[8:])
-        return tuple(v.reshape(nz, ROWS, COLS) for v in out)
+        flat = [v.transpose(1, 2, 0) for v in args[:8]]
+        out = call(ns, nt, args[0].shape[0], consts, *flat, *args[8:])
+        return tuple(v.transpose(2, 0, 1) for v in out)
 
     block = P(None, "ys", "xs")
     return jax.shard_map(

time: 71.9 us -> 59 us (0.82)
  local copies, waits for them, and re-layouts: 13.3 us -> 6.27 us
  Pallas kernels: 57.3 us -> 51.8 us
    unnamed x40 -> x4, local copies, waits for them, and re-layouts: 13.3 us -> 6.27 us
    pallas_call x1, Pallas kernels: 57.3 us -> 51.8 us  [call(): pl.pallas_call(functools.partial(kernel, ns, nt, nz, places), out_shape=[...]
where the time goes in v1:
time: 59 us; the launch traced here: 58.8 us
  Pallas kernels  51.8 us (88%)
  local copies, waits for them, and re-layouts  6.27 us (11%)
  between operations  0.65 us (1%)
    pallas_call x1, Pallas kernels, call(): pl.pallas_call(functools.partial(kernel, ns, nt, nz, places), out_shape=[...  51.8 us
    unnamed x4, local copies, waits for them, and re-layouts  6.27 us

profile of v1, /device:TPU:1, one launch (start us, length us, event | category | flops | bytes accessed | tf_op | source)
XLA Modules:
  0.0 58.8 jit_solution(11559664135354314499)
XLA Ops:
  0.6 51.8 %shard_map.165 = (f32[8,32,48]{2,1,0:T(8,128)}, f32[8,32,48]{2,1,0:T(8,128)}, f32[8,32,48]{2,1,0:T(8,128)}, f32[8,32,48]{2,1,0:T(8,128)}) custom-call(f32[8,32,48]{2,1,0:T(8,128)} %bitcast.12, f32[8,32,48]{2,1,0:T(8,128)} %bitcast.13, f32[8,32,48]{2,1,0:T(8,128)} %bitcast.14, f32[8,32,48]{2,1,0:T(8,128)} %bitcast.15, f32[8,32,48]{2,1,0:T(8,128)} %bitcast.16, ...), custom_call_target="tpu_custom_call" | custom-call | tf_op jit(solution)/shard_map/pallas_call | solution.py:630
  52.5 1.6 %copy.22 = f32[48,8,32]{0,2,1:T(8,128)} copy(f32[48,8,32]{0,2,1:T(8,128)} %bitcast.23) | data formatting | bytes 98304
  54.1 1.6 %copy.23 = f32[48,8,32]{0,2,1:T(8,128)} copy(f32[48,8,32]{0,2,1:T(8,128)} %bitcast.22) | data formatting | bytes 98304
  55.6 1.6 %copy.24 = f32[48,8,32]{0,2,1:T(8,128)} copy(f32[48,8,32]{0,2,1:T(8,128)} %bitcast.21) | data formatting | bytes 98304
  57.2 1.6 %copy.25 = f32[48,8,32]{0,2,1:T(8,128)} copy(f32[48,8,32]{0,2,1:T(8,128)} %bitcast.20) | data formatting | bytes 98304

commit v2 on v1

--- a/solution.py
+++ b/solution.py
@@ -617,6 +617,17 @@
             loads[8].wait()
 
 
+def hand_over(a, b, c, d, out_a, out_b, out_c, out_d, sem):
+    copies = [
+        pltpu.make_async_copy(src, dst, sem.at[n])
+        for n, (src, dst) in enumerate(((a, out_a), (b, out_b), (c, out_c), (d, out_d)))
+    ]
+    for copy in copies:
+        copy.start()
+    for copy in copies:
+        copy.wait()
+
+
 def call(ns, nt, nz, consts, *args):
     ng = nz // 2
     packed, spectral, places = consts
@@ -627,7 +638,7 @@
         return pltpu.VMEM(shape, F32)
 
     out = jax.ShapeDtypeStruct((ROWS, COLS, nz), F32)
-    return pl.pallas_call(
+    made = pl.pallas_call(
         functools.partial(kernel, ns, nt, nz, places),
         out_shape=[out] * 4,
         in_specs=[anywhere] * 11 + [smem] + [anywhere] * 2,
@@ -650,6 +661,13 @@
             collective_id=0, has_side_effects=True, vmem_limit_bytes=60 * 1024 * 1024
         ),
     )(*args, jnp.asarray(packed), jnp.asarray(spectral))
+    return pl.pallas_call(
+        hand_over,
+        out_shape=[out] * 4,
+        in_specs=[anywhere] * 4,
+        out_specs=[anywhere] * 4,
+        scratch_shapes=[pltpu.SemaphoreType.DMA((4,))],
+    )(*made)
 
 
 def solution(mesh):

time: 59 us -> 69.7 us (1.18)
  Pallas kernels: 51.8 us -> 68.9 us
  local copies, waits for them, and re-layouts: 6.27 us -> 0 us
    pallas_call x0 -> x1, Pallas kernels: none -> 17 us  [call(): pl.pallas_call(hand_over, out_shape=[out] * 4, in_specs=[anywhere] * 4, o...]
    unnamed x4 -> x0, local copies, waits for them, and re-layouts: 6.27 us -> none
where the time goes in v2:
time: 69.7 us; the launch traced here: 69.5 us
  Pallas kernels  68.9 us (99%)
    pallas_call x1, Pallas kernels, call(): pl.pallas_call(functools.partial(kernel, ns, nt, nz, places), out_shape=[...  51.8 us
    pallas_call x1, Pallas kernels, call(): pl.pallas_call(hand_over, out_shape=[out] * 4, in_specs=[anywhere] * 4, o...  17 us

profile of v2, /device:TPU:1, one launch (start us, length us, event | category | flops | bytes accessed | tf_op | source)
XLA Modules:
  0.0 69.5 jit_solution(17520382498572849441)
XLA Ops:
  0.6 51.8 %shard_map.165 = (f32[8,32,48]{2,1,0:T(8,128)}, f32[8,32,48]{2,1,0:T(8,128)}, f32[8,32,48]{2,1,0:T(8,128)}, f32[8,32,48]{2,1,0:T(8,128)}) custom-call(f32[8,32,48]{2,1,0:T(8,128)} %bitcast.12, f32[8,32,48]{2,1,0:T(8,128)} %bitcast.13, f32[8,32,48]{2,1,0:T(8,128)} %bitcast.14, f32[8,32,48]{2,1,0:T(8,128)} %bitcast.15, f32[8,32,48]{2,1,0:T(8,128)} %bitcast.16, ...), custom_call_target="tpu_custom_call" | custom-call | tf_op jit(solution)/shard_map/pallas_call | solution.py:641
  52.5 17.0 %shard_map.166 = (f32[8,32,48]{2,1,0:T(8,128)}, f32[8,32,48]{2,1,0:T(8,128)}, f32[8,32,48]{2,1,0:T(8,128)}, f32[8,32,48]{2,1,0:T(8,128)}) custom-call(f32[8,32,48]{2,1,0:T(8,128)} %get-tuple-element.12.a, f32[8,32,48]{2,1,0:T(8,128)} %get-tuple-element.13.b, f32[8,32,48]{2,1,0:T(8,128)} %get-tuple-element.14.c, f32[8,32,48]{2,1,0:T(8,128)} %get-tuple-element.15.d), custom_call_target="tpu_custom_call" | custom-call | tf_op jit(solution)/shard_map/pallas_call | solution.py:664

commit v3 on v1

--- a/solution.py
+++ b/solution.py
@@ -101,6 +101,15 @@
         return (late == 0) | ((y + 2) % 8 < 4)
 
     return index_of, pair_of, has
+
+
+def partner(t, i, nt):
+    if nt != 32:
+        return lax.rem(t + 1 + i, nt)
+    flip, k, turn = (31 - i) // 16, (i % 16) // 2, 1 - i % 2
+    odd = k % 2
+    step = 4 + (1 - odd) * (k // 2) - odd * ((k + 1) // 2)
+    return (t // 4 + step) % 8 * 4 + (t // 2 + flip) % 2 * 2 + (t + turn) % 2
 
 
 def dot(a, b):
@@ -172,11 +181,11 @@
 def kernel(
     ns, nt, nz, places,
     fu_h, fv_h, fw_h, fc_h, iu_h, iv_h, iw_h, it_h, dinv_h, vecs_h, minv_h, eig, packed_h, spec_h,
-    out_u, out_v, out_w, out_c,
+    ou, ov, ow, oc,
     raw, mats, packed, spec, rhs, u10, v14, w10, c18, iu10, iv10, iw14, it14, modal,
     xe, xw, xfw, xfe, yn2, ys2, yfs2, yfn2,
     s1, r1, s2, r2, s3, r3, s4, r4,
-    ax, wx, ay, wy, ch, d_buf, p_buf, mw_buf, ou, ov, ow, oc,
+    ax, wx, ay, wy, ch, d_buf, p_buf, mw_buf,
     in_sem, h_send, h_recv, p_send, p_recv, ready,
 ):
     ng = nz // 2
@@ -334,16 +343,15 @@
             pl.semaphore_wait(barrier, ng + 3)
 
     def send1(i, _):
-        g = lax.rem(t + i, ng)
-        to = index_of(g)
-
-        @pl.when(to != t)
+        to = partner(t, i, nt)
+
+        @pl.when(has(to))
         def _():
-            remote(s1.at[rows(g, 8)], r1.at[rows(t, 8)], s, to, p_send.at[0], p_recv.at[0]).start()
+            remote(s1.at[rows(pair_of(to), 8)], r1.at[rows(t, 8)], s, to, p_send.at[0], p_recv.at[0]).start()
 
         return 0
 
-    lax.fori_loop(0, ng, send1, 0)
+    lax.fori_loop(0, nt - 1, send1, 0)
 
     @pl.when(owner)
     def _():
@@ -530,11 +538,11 @@
         s4[pl.ds(7, nt, stride=8), :] = edge
 
         def send4(i, _):
-            g = lax.rem(t + i, nt)
+            g = partner(t, i, nt)
             remote(s4.at[rows(g, 8)], r4.at[rows(mine, 8)], s, g, p_send.at[3], p_recv.at[3]).start()
             return 0
 
-        lax.fori_loop(1, nt, send4, 0)
+        lax.fori_loop(0, nt - 1, send4, 0)
         pltpu.make_async_copy(s4.at[rows(t, 8)], r4.at[rows(mine, 8)], p_recv.at[3]).start()
 
     c10, w = c18[:, 256:896], w10[...]
@@ -592,14 +600,6 @@
 
     lax.fori_loop(0, nz // 8, last, 0)
 
-    for src, dst in ((ou, out_u), (ov, out_v), (ow, out_w), (oc, out_c)):
-        for k in range(5):
-            v = src[:, tile(k)].T
-            if k > 0:
-                dst[2 * k - 1] = v[8:40]
-            if k < 4:
-                dst[2 * k] = v[72:104]
-
     for copy in halos:
         copy.wait_send()
 
@@ -617,6 +617,21 @@
             loads[8].wait()
 
 
+def finish(a, b, c, d, out_a, out_b, out_c, out_d, made, sem):
+    copies = []
+    for n, (src, dst) in enumerate(((a, out_a), (b, out_b), (c, out_c), (d, out_d))):
+        for k in range(5):
+            v = src[:, 128 * k : 128 * k + 128].T
+            if k > 0:
+                made[n, 2 * k - 1] = v[8:40]
+            if k < 4:
+                made[n, 2 * k] = v[72:104]
+        copies.append(pltpu.make_async_copy(made.at[n], dst, sem.at[n]))
+        copies[n].start()
+    for copy in copies:
+        copy.wait()
+
+
 def call(ns, nt, nz, consts, *args):
     ng = nz // 2
     packed, spectral, places = consts
@@ -627,9 +642,9 @@
         return pltpu.VMEM(shape, F32)
 
     out = jax.ShapeDtypeStruct((ROWS, COLS, nz), F32)
-    return pl.pallas_call(
+    made = pl.pallas_call(
         functools.partial(kernel, ns, nt, nz, places),
-        out_shape=[out] * 4,
+        out_shape=[pltpu.VMEM((nz, 640), F32)] * 4,
         in_specs=[anywhere] * 11 + [smem] + [anywhere] * 2,
         out_specs=[vmem] * 4,
         scratch_shapes=[
@@ -642,7 +657,6 @@
             buf(16 * ns, 128), buf(16 * ns, 128), buf(8 * nt, 128), buf(8 * ng, 128),
             buf(6, nz, 640), buf(nz, 640), buf(6, nz, 896), buf(nz, 896), buf(2, nz, 640),
             buf(nz, 896), buf(nz, 896), buf(nz, 640),
-            buf(nz, 640), buf(nz, 640), buf(nz, 640), buf(nz, 640),
             pltpu.SemaphoreType.DMA((13,)), pltpu.SemaphoreType.DMA((4,)), pltpu.SemaphoreType.DMA((4,)),
             pltpu.SemaphoreType.DMA((4,)), pltpu.SemaphoreType.DMA((4,)), pltpu.SemaphoreType.REGULAR,
         ],
@@ -650,6 +664,13 @@
             collective_id=0, has_side_effects=True, vmem_limit_bytes=60 * 1024 * 1024
         ),
     )(*args, jnp.asarray(packed), jnp.asarray(spectral))
+    return pl.pallas_call(
+        finish,
+        out_shape=[out] * 4,
+        in_specs=[vmem] * 4,
+        out_specs=[anywhere] * 4,
+        scratch_shapes=[buf(4, ROWS, COLS, nz), pltpu.SemaphoreType.DMA((4,))],
+    )(*[pltpu.with_memory_space_constraint(v, pltpu.VMEM) for v in made])
 
 
 def solution(mesh):

time: 59 us -> 51.6 us (0.87)
  local copies, waits for them, and re-layouts: 6.27 us -> 0 us
  Pallas kernels: 51.8 us -> 50.8 us
    unnamed x4 -> x0, local copies, waits for them, and re-layouts: 6.27 us -> none
    pallas_call x1, Pallas kernels: 51.8 us -> 49.8 us  [call(): pl.pallas_call(functools.partial(kernel, ns, nt, nz, places), out_shape=[...]
    pallas_call x0 -> x1, Pallas kernels: none -> 1.01 us  [call(): pl.pallas_call(finish, out_shape=[out] * 4, in_specs=[vmem] * 4, out_spec...]
where the time goes in v3:
time: 51.6 us; the launch traced here: 51.5 us
  Pallas kernels  50.8 us (98%)
  between operations  0.64 us (1%)
    pallas_call x1, Pallas kernels, call(): pl.pallas_call(functools.partial(kernel, ns, nt, nz, places), out_shape=[...  49.8 us

profile of v3, /device:TPU:1, one launch (start us, length us, event | category | flops | bytes accessed | tf_op | source)
XLA Modules:
  0.0 51.5 jit_solution(8168056286372615224)
XLA Ops:
  0.6 49.8 %shard_map.165 = (f32[48,640]{1,0:T(8,128)S(1)}, f32[48,640]{1,0:T(8,128)S(1)}, f32[48,640]{1,0:T(8,128)S(1)}, f32[48,640]{1,0:T(8,128)S(1)}) custom-call(f32[8,32,48]{2,1,0:T(8,128)} %bitcast.12, f32[8,32,48]{2,1,0:T(8,128)} %bitcast.13, f32[8,32,48]{2,1,0:T(8,128)} %bitcast.14, f32[8,32,48]{2,1,0:T(8,128)} %bitcast.15, f32[8,32,48]{2,1,0:T(8,128)} %bitcast.16, ...), custom_call_target="tpu_custom_call" | custom-call | tf_op jit(solution)/shard_map/pallas_call | solution.py:645
  50.4 1.0 %shard_map.166 = (f32[8,32,48]{2,1,0:T(8,128)}, f32[8,32,48]{2,1,0:T(8,128)}, f32[8,32,48]{2,1,0:T(8,128)}, f32[8,32,48]{2,1,0:T(8,128)}) custom-call(f32[48,640]{1,0:T(8,128)S(1)} %get-tuple-element.12.a, f32[48,640]{1,0:T(8,128)S(1)} %get-tuple-element.13.b, f32[48,640]{1,0:T(8,128)S(1)} %get-tuple-element.14.c, f32[48,640]{1,0:T(8,128)S(1)} %get-tuple-element.15.d), custom_call_target="tpu_custom_call" | custom-call | tf_op jit(solution)/shard_map/pallas_call | solution.py:667

commit v4 on v3

--- a/solution.py
+++ b/solution.py
@@ -106,10 +106,9 @@
 def partner(t, i, nt):
     if nt != 32:
         return lax.rem(t + 1 + i, nt)
-    flip, k, turn = (31 - i) // 16, (i % 16) // 2, 1 - i % 2
-    odd = k % 2
-    step = 4 + (1 - odd) * (k // 2) - odd * ((k + 1) // 2)
-    return (t // 4 + step) % 8 * 4 + (t // 2 + flip) % 2 * 2 + (t + turn) % 2
+    flip, step, turn = (31 - i) // 16, (4, 3, 5, 2, 6, 1, 7, 0)[i % 16 // 2], 1 - i % 2
+    y, z, core = lax.div(t, 4), lax.rem(lax.div(t, 2), 2), lax.rem(t, 2)
+    return 4 * lax.rem(y + step, 8) + 2 * lax.rem(z + flip, 2) + lax.rem(core + turn, 2)
 
 
 def dot(a, b):
@@ -185,7 +184,7 @@
     raw, mats, packed, spec, rhs, u10, v14, w10, c18, iu10, iv10, iw14, it14, modal,
     xe, xw, xfw, xfe, yn2, ys2, yfs2, yfn2,
     s1, r1, s2, r2, s3, r3, s4, r4,
-    ax, wx, ay, wy, ch, d_buf, p_buf, mw_buf,
+    ax, wx, ay, wy, ch, d_buf, vert,
     in_sem, h_send, h_recv, p_send, p_recv, ready,
 ):
     ng = nz // 2
@@ -196,36 +195,6 @@
     mine = pair_of(t)
     late = nt - ng
 
-    barrier = pltpu.get_barrier_semaphore()
-
-    def greet(a, b):
-        pl.semaphore_signal(barrier, 1, device_id=(a, b), device_id_type=MESH)
-
-    def greet_x(i, _):
-        greet(s, lax.rem(t + i, nt))
-        return 0
-
-    def greet_y(i, _):
-        greet(lax.rem(s + i, ns), t)
-        return 0
-
-    east, west = lax.rem(t + 1, nt), lax.rem(t + nt - 1, nt)
-    north, south = lax.rem(s + 1, ns), lax.rem(s + ns - 1, ns)
-    twin = t + 1 - 2 * lax.rem(t, 2)
-
-    @pl.when(owner)
-    def _():
-        lax.fori_loop(1, nt, greet_x, 0)
-        lax.fori_loop(1, ns, greet_y, 0)
-
-    if late:
-
-        @pl.when(other)
-        def _():
-            greet(north, t)
-            greet(south, t)
-            greet(s, twin)
-
     loads = []
     for n, src in enumerate((iu_h, iv_h, iw_h, it_h, fc_h, fu_h, fv_h, fw_h)):
         dst = raw.at[n, pl.ds(1, ROWS), pl.ds(8, COLS)]
@@ -234,9 +203,33 @@
     loads.append(pltpu.make_async_copy(packed_h, packed, in_sem.at[9]))
     for n, src in enumerate((vecs_h, minv_h, dinv_h)):
         loads.append(pltpu.make_async_copy(src, mats.at[n], in_sem.at[10 + n]))
-    order = (0, 1, 2, 10, 9, 8, 3, 4, 5, 6, 7, 11, 12)
+    order = (10, 0, 1, 2, 9, 8, 3, 4, 5, 6, 7, 11, 12)
     for n in order:
         loads[n].start()
+
+    barrier = pltpu.get_barrier_semaphore()
+
+    def greet(a, b):
+        pl.semaphore_signal(barrier, 1, device_id=(a, b), device_id_type=MESH)
+
+    east, west = lax.rem(t + 1, nt), lax.rem(t + nt - 1, nt)
+    north, south = lax.rem(s + 1, ns), lax.rem(s + ns - 1, ns)
+    twin = t + 1 - 2 * lax.rem(t, 2)
+
+    @pl.when(owner)
+    def _():
+        for i in range(nt - 1):
+            greet(s, partner(t, i, nt))
+        for i in range(1, ns):
+            greet(lax.rem(s + i, ns), t)
+
+    if late:
+
+        @pl.when(other)
+        def _():
+            greet(north, t)
+            greet(south, t)
+            greet(s, twin)
 
     lane = lax.broadcasted_iota(jnp.int32, (nz, 128), 1)
     slot = lane & 63
@@ -342,16 +335,13 @@
         def _():
             pl.semaphore_wait(barrier, ng + 3)
 
-    def send1(i, _):
-        to = partner(t, i, nt)
-
+    def send1(to):
         @pl.when(has(to))
         def _():
             remote(s1.at[rows(pair_of(to), 8)], r1.at[rows(t, 8)], s, to, p_send.at[0], p_recv.at[0]).start()
 
-        return 0
-
-    lax.fori_loop(0, nt - 1, send1, 0)
+    for i in range(nt - 1):
+        send1(partner(t, i, nt))
 
     @pl.when(owner)
     def _():
@@ -385,6 +375,14 @@
         ys2[3 + n] = pair(iw14[:, tile(1 + n)], it14[:, tile(1 + n)])
     yn2[5] = pair(iu10[:, tile(4)], iv10[:, tile(4)])
     ys2[5] = pair(iu10[:, tile(0)], iv10[:, tile(0)])
+    halos = [
+        remote(xe, xfw, s, east, h_send.at[0], h_recv.at[0]),
+        remote(yn2, yfs2, north, t, h_send.at[1], h_recv.at[1]),
+        remote(xw, xfe, s, west, h_send.at[2], h_recv.at[2]),
+        remote(ys2, yfn2, south, t, h_send.at[3], h_recv.at[3]),
+    ]
+    halos[1].start()
+    halos[3].start()
     loads[9].wait()
 
     @pl.when(owner)
@@ -403,12 +401,9 @@
         for i in range(9, 16):
             s2[pl.ds(i, ns, stride=16), :] = jnp.zeros((ns, 128), F32)
 
-        def send2(i, _):
+        for i in range(1, ns):
             j = lax.rem(s + i, ns)
             remote(s2.at[rows(j, 16)], r2.at[rows(s, 16)], j, t, p_send.at[1], p_recv.at[1]).start()
-            return 0
-
-        lax.fori_loop(1, ns, send2, 0)
         pltpu.make_async_copy(s2.at[rows(s, 16)], r2.at[rows(s, 16)], p_recv.at[1]).start()
 
     if late:
@@ -417,14 +412,8 @@
         def _():
             pl.semaphore_wait(ready, late)
 
-    halos = [
-        remote(xe, xfw, s, east, h_send.at[0], h_recv.at[0]),
-        remote(yn2, yfs2, north, t, h_send.at[1], h_recv.at[1]),
-        remote(xw, xfe, s, west, h_send.at[2], h_recv.at[2]),
-        remote(ys2, yfn2, south, t, h_send.at[3], h_recv.at[3]),
-    ]
-    for copy in halos:
-        copy.start()
+    halos[0].start()
+    halos[2].start()
 
     @pl.when(owner)
     def _():
@@ -450,14 +439,12 @@
         y = dot(table(1), dot_nt(y, inner))
         s3[...] = y
 
-        def send3(i, _):
+        for i in range(1, ns):
             j = lax.rem(s + i, ns)
             remote(s3.at[rows(j, 16)], r3.at[rows(s, 16)], j, t, p_send.at[2], p_recv.at[2]).start()
-            return 0
-
-        lax.fori_loop(1, ns, send3, 0)
         pltpu.make_async_copy(s3.at[rows(s, 16)], r3.at[rows(s, 16)], p_recv.at[2]).start()
 
+    diffusion = (0.0, 0.0, KAPPA, -KAPPA, 0.0, 0.0)
     halos[0].wait_recv()
     unpack_x(xfw, ((iw14, 1, -3, 0, 3), (it14, 1, -3, 3, 3), (iu10, 0, -1, 6, 1), (iv10, 0, -1, 7, 1), (u10, 0, -3, 8, 3), (c18, 2, -5, 11, 5)))
     halos[2].wait_recv()
@@ -466,9 +453,9 @@
     def x_faces(n, _):
         at = pl.ds(pl.multiple_of(8 * n, 8), 8)
         value, parts = weno_parts(c18[at, 256:896], u10[at, :], 1, lambda f: f)
-        wx[at, :] = value
+        wx[at, :] = DT * value
         for o in range(6):
-            ax[o, at, :] = parts[o]
+            ax[o, at, :] = roll(DT * (parts[o] + diffusion[o]), o - 2)
         return 0
 
     lax.fori_loop(0, nz // 8, x_faces, 0)
@@ -501,9 +488,9 @@
     def y_faces(n, _):
         at = pl.ds(pl.multiple_of(8 * n, 8), 8)
         value, parts = weno_parts(c18[at, :], v14[at, :], 64, lambda f: f[:, 128:1024])
-        wy[at, :] = value
+        wy[at, :] = DT * value[:, 128:768]
         for o in range(6):
-            ay[o, at, :] = parts[o]
+            ay[o, at, :] = roll(DT * (parts[o] + diffusion[o]), 64 * (o - 2))[:, 128:768]
         return 0
 
     lax.fori_loop(0, nz // 8, y_faces, 0)
@@ -537,68 +524,71 @@
                 edge = jnp.where((at >= 16 + k) & (at < 19 + k), roll(after[:, tile(i)], 16 + k), edge)
         s4[pl.ds(7, nt, stride=8), :] = edge
 
-        def send4(i, _):
+        for i in range(nt - 1):
             g = partner(t, i, nt)
             remote(s4.at[rows(g, 8)], r4.at[rows(mine, 8)], s, g, p_send.at[3], p_recv.at[3]).start()
-            return 0
-
-        lax.fori_loop(0, nt - 1, send4, 0)
         pltpu.make_async_copy(s4.at[rows(t, 8)], r4.at[rows(mine, 8)], p_recv.at[3]).start()
 
-    c10, w = c18[:, 256:896], w10[...]
-    ch[0] = jnp.where(level == nz - 1, 0.0, 0.5 * (c10 + roll(c10, -1, 0)))
-    ch[1] = jnp.where(level == nz - 1, 0.0, 0.5 * w)
-
+    c10 = c18[:, 256:896]
+    ch[0] = jnp.where(level == nz - 1, 0.0, 0.5 * DT * (c10 + roll(c10, -1, 0)))
+    ch[1] = jnp.where(level == nz - 1, 0.0, 0.5 * DT * w10[...])
+    iw = iw14[:, 128:768]
+    it14[...] = it14[...] + GRAV * DT * iw14[...]
+    w10[...] = iw + DT * NU * spread(iw)
+    iu10[...] = iu10[...] + DT * NU * spread(iu10[...])
+    iv10[...] = iv10[...] + DT * NU * spread(iv10[...])
     loads[11].wait()
     loads[12].wait()
+    vert[0] = jnp.concatenate([mats[1, pl.ds(0, ng, stride=2), :], mats[1, pl.ds(1, ng, stride=2), :]], 0).T
+    vert[1] = mats[2].T
+
     pltpu.make_async_copy(r4, r4, p_recv.at[3]).wait()
     cols = []
     for i in range(8):
         one = r4[pl.ds(i, ng, stride=8), :]
-        modal[i, pl.ds(0, ng, stride=2), :] = roll(one, 8)
-        modal[i, pl.ds(1, ng, stride=2), :] = roll(one, -24)
-        cols.append(modal[i])
-    p = dot_tn(mats[1], jnp.concatenate(cols, 1))
+        cols.append(jnp.concatenate([roll(one, 8), roll(one, -24)], 0))
+    p = dot(vert[0], jnp.concatenate(cols, 1))
     edge = p[:, tile(7)]
+    cols = []
     for i in range(7):
         v = p[:, tile(i)]
         if 1 <= i <= 5:
             k = 3 * (i - 1)
             v = jnp.where((slot >= 5) & (slot < 8), roll(edge, -3 - k), v)
             v = jnp.where((slot >= 40) & (slot < 43), roll(edge, 16 - k), v)
-        p_buf[:, tile(i)] = v
-    p = p_buf[...]
-    upper = jnp.where(lax.broadcasted_iota(jnp.int32, p.shape, 0) == nz - 1, 0.0, roll(p, -1, 0))
-    mid = iw14[...] - (upper - p)
-    mw_buf[...] = mid[:, 128:768]
-    d = dot_tn(mats[2], it14[...] + GRAV * DT * mid)
-    d_buf[...] = d
-    d10 = d[:, 128:768]
+        cols.append(v)
+    p = jnp.concatenate(cols, 1)
+    top = lax.broadcasted_iota(jnp.int32, p.shape, 0) == nz - 1
+    upper = jnp.where(top, 0.0, roll(p, -1, 0))
+    d_buf[...] = dot(vert[1], it14[...] - GRAV * DT * (upper - p))
+    p = p + DT * NU * spread(p)
+    p10 = p[:, 128:768]
+    ow[...] = w10[...] - (jnp.where(level == nz - 1, 0.0, roll(p10, -1, 0)) - p10)
+    ou[...] = iu10[...] - (roll(p10, -1) - p10)
+    ov[...] = iv10[...] - (roll(p, -64)[:, 128:768] - p10)
+    d10 = d_buf[:, 128:768]
     gz = roll(d10, -1, 0) - d10
     wz = ch[1] * gz
-    oc[...] = d10 + DT * (wz + roll(wz, 1, 0))
-    mw = mw_buf[...]
-    ow[...] = mw + DT * NU * spread(mw) + DT * (ch[0] * gz)
-
-    def last(n, _):
-        at = pl.ds(pl.multiple_of(8 * n, 8), 8)
-        p14, d14 = p_buf[at, :], d_buf[at, :]
-        p10, dx = p14[:, 128:768], d14[:, 128:768]
-        mu = iu10[at, :] - (roll(p10, -1) - p10)
-        mv = iv10[at, :] - (roll(p14, -64)[:, 128:768] - p10)
+    oc[...] = d10 + (wz + roll(wz, 1, 0))
+    ow[...] = ow[...] + ch[0] * gz
+
+    for n in range(nz // 8):
+        at = slice(8 * n, 8 * n + 8)
+        d14 = d_buf[at, :]
+        dx = d14[:, 128:768]
         gx = roll(dx, -1) - dx
-        gy = roll(d14, -64) - d14
-        total = KAPPA * spread(dx)
-        ty = jnp.zeros_like(d14)
+        ahead = roll(d14, -64)
+        gy, gy_back = ahead - d14, d14 - roll(d14, 64)
+        total = oc[at, :]
         for o in range(6):
-            total = total + roll(ax[o, at, :] * gx, o - 2)
-            ty = ty + roll(ay[o, at, :] * gy, 64 * (o - 2))
-        ou[at, :] = mu + DT * NU * spread(mu) + DT * (wx[at, :] * gx)
-        ov[at, :] = mv + DT * NU * spread(mv) + DT * (wy[at, :] * gy)[:, 128:768]
-        oc[at, :] = oc[at, :] + DT * (total + ty[:, 128:768])
-        return 0
-
-    lax.fori_loop(0, nz // 8, last, 0)
+            total = total + ax[o, at, :] * roll(gx, o - 2)
+            first = 128 - 64 * (o - 2)
+            g = gy if o % 2 == 0 else gy_back
+            first = first if o % 2 == 0 else first + 64
+            total = total + ay[o, at, :] * g[:, first : first + 640]
+        ou[at, :] = ou[at, :] + wx[at, :] * gx
+        ov[at, :] = ov[at, :] + wy[at, :] * gy[:, 128:768]
+        oc[at, :] = total
 
     for copy in halos:
         copy.wait_send()
@@ -655,8 +645,8 @@
             buf(6, nz, 128), buf(6, nz, 128), buf(6, nz, 128), buf(6, nz, 128),
             buf(8 * ng, 128), buf(8 * nt, 128), buf(16 * ns, 128), buf(16 * ns, 128),
             buf(16 * ns, 128), buf(16 * ns, 128), buf(8 * nt, 128), buf(8 * ng, 128),
-            buf(6, nz, 640), buf(nz, 640), buf(6, nz, 896), buf(nz, 896), buf(2, nz, 640),
-            buf(nz, 896), buf(nz, 896), buf(nz, 640),
+            buf(6, nz, 640), buf(nz, 640), buf(6, nz, 640), buf(nz, 640), buf(2, nz, 640),
+            buf(nz, 896), buf(2, nz, nz),
             pltpu.SemaphoreType.DMA((13,)), pltpu.SemaphoreType.DMA((4,)), pltpu.SemaphoreType.DMA((4,)),
             pltpu.SemaphoreType.DMA((4,)), pltpu.SemaphoreType.DMA((4,)), pltpu.SemaphoreType.REGULAR,
         ],

time: 51.6 us -> 47.7 us (0.924)
  Pallas kernels: 50.8 us -> 46.9 us
    pallas_call x1, Pallas kernels: 49.8 us -> 45.9 us  [call(): pl.pallas_call(functools.partial(kernel, ns, nt, nz, places), out_shape=[...]
where the time goes in v4:
time: 47.7 us; the launch traced here: 47.5 us
  Pallas kernels  46.9 us (98%)
  between operations  0.64 us (1%)
    pallas_call x1, Pallas kernels, call(): pl.pallas_call(functools.partial(kernel, ns, nt, nz, places), out_shape=[...  45.9 us
    pallas_call x1, Pallas kernels, call(): pl.pallas_call(finish, out_shape=[out] * 4, in_specs=[vmem] * 4, out_spec...  1.01 us

profile of v4, /device:TPU:1, one launch (start us, length us, event | category | flops | bytes accessed | tf_op | source)
XLA Modules:
  0.0 47.5 jit_solution(295182204436150791)
XLA Ops:
  0.6 45.9 %shard_map.165 = (f32[48,640]{1,0:T(8,128)S(1)}, f32[48,640]{1,0:T(8,128)S(1)}, f32[48,640]{1,0:T(8,128)S(1)}, f32[48,640]{1,0:T(8,128)S(1)}) custom-call(f32[8,32,48]{2,1,0:T(8,128)} %bitcast.12, f32[8,32,48]{2,1,0:T(8,128)} %bitcast.13, f32[8,32,48]{2,1,0:T(8,128)} %bitcast.14, f32[8,32,48]{2,1,0:T(8,128)} %bitcast.15, f32[8,32,48]{2,1,0:T(8,128)} %bitcast.16, ...), custom_call_target="tpu_custom_call" | custom-call | tf_op jit(solution)/shard_map/pallas_call | solution.py:635
  46.5 1.0 %shard_map.166 = (f32[8,32,48]{2,1,0:T(8,128)}, f32[8,32,48]{2,1,0:T(8,128)}, f32[8,32,48]{2,1,0:T(8,128)}, f32[8,32,48]{2,1,0:T(8,128)}) custom-call(f32[48,640]{1,0:T(8,128)S(1)} %get-tuple-element.12.a, f32[48,640]{1,0:T(8,128)S(1)} %get-tuple-element.13.b, f32[48,640]{1,0:T(8,128)S(1)} %get-tuple-element.14.c, f32[48,640]{1,0:T(8,128)S(1)} %get-tuple-element.15.d), custom_call_target="tpu_custom_call" | custom-call | tf_op jit(solution)/shard_map/pallas_call | solution.py:657

commit v5 on v4

--- a/solution.py
+++ b/solution.py
@@ -179,12 +179,12 @@
 
 def kernel(
     ns, nt, nz, places,
-    fu_h, fv_h, fw_h, fc_h, iu_h, iv_h, iw_h, it_h, dinv_h, vecs_h, minv_h, eig, packed_h, spec_h,
+    fu_h, fv_h, fw_h, fc_h, iu_h, iv_h, iw_h, it_h, dinv_h, vecs_h, minv_h, eig_h, packed_h, spec_h,
     ou, ov, ow, oc,
-    raw, mats, packed, spec, rhs, u10, v14, w10, c18, iu10, iv10, iw14, it14, modal,
+    eig, raw, mats, packed, spec, rhs, u10, v14, w10, c18, iu10, iv10, iw14, it14, modal,
     xe, xw, xfw, xfe, yn2, ys2, yfs2, yfn2,
     s1, r1, s2, r2, s3, r3, s4, r4,
-    ax, wx, ay, wy, ch, d_buf, vert,
+    ax, wx, ay, wy, ch, d_buf, vert, yfwd,
     in_sem, h_send, h_recv, p_send, p_recv, ready,
 ):
     ng = nz // 2
@@ -195,6 +195,30 @@
     mine = pair_of(t)
     late = nt - ng
 
+    barrier = pltpu.get_barrier_semaphore()
+
+    def greet(a, b):
+        pl.semaphore_signal(barrier, 1, device_id=(a, b), device_id_type=MESH)
+
+    east, west = lax.rem(t + 1, nt), lax.rem(t + nt - 1, nt)
+    north, south = lax.rem(s + 1, ns), lax.rem(s + ns - 1, ns)
+    twin = t + 1 - 2 * lax.rem(t, 2)
+
+    @pl.when(owner)
+    def _():
+        for i in range(nt - 1):
+            greet(s, partner(t, i, nt))
+        for i in range(1, ns):
+            greet(lax.rem(s + i, ns), t)
+
+    if late:
+
+        @pl.when(other)
+        def _():
+            greet(north, t)
+            greet(south, t)
+            greet(s, twin)
+
     loads = []
     for n, src in enumerate((iu_h, iv_h, iw_h, it_h, fc_h, fu_h, fv_h, fw_h)):
         dst = raw.at[n, pl.ds(1, ROWS), pl.ds(8, COLS)]
@@ -203,33 +227,10 @@
     loads.append(pltpu.make_async_copy(packed_h, packed, in_sem.at[9]))
     for n, src in enumerate((vecs_h, minv_h, dinv_h)):
         loads.append(pltpu.make_async_copy(src, mats.at[n], in_sem.at[10 + n]))
-    order = (10, 0, 1, 2, 9, 8, 3, 4, 5, 6, 7, 11, 12)
+    loads.append(pltpu.make_async_copy(eig_h, eig, in_sem.at[13]))
+    order = (10, 0, 1, 2, 9, 8, 3, 4, 5, 6, 7, 11, 12, 13)
     for n in order:
         loads[n].start()
-
-    barrier = pltpu.get_barrier_semaphore()
-
-    def greet(a, b):
-        pl.semaphore_signal(barrier, 1, device_id=(a, b), device_id_type=MESH)
-
-    east, west = lax.rem(t + 1, nt), lax.rem(t + nt - 1, nt)
-    north, south = lax.rem(s + 1, ns), lax.rem(s + ns - 1, ns)
-    twin = t + 1 - 2 * lax.rem(t, 2)
-
-    @pl.when(owner)
-    def _():
-        for i in range(nt - 1):
-            greet(s, partner(t, i, nt))
-        for i in range(1, ns):
-            greet(lax.rem(s + i, ns), t)
-
-    if late:
-
-        @pl.when(other)
-        def _():
-            greet(north, t)
-            greet(south, t)
-            greet(s, twin)
 
     lane = lax.broadcasted_iota(jnp.int32, (nz, 128), 1)
     slot = lane & 63
@@ -238,8 +239,12 @@
     lane_g = lax.broadcasted_iota(jnp.int32, (ng, 128), 1)
     level = lax.broadcasted_iota(jnp.int32, (nz, 640), 0)
 
-    def rows(n, count):
-        return pl.ds(pl.multiple_of(n * count, count), count)
+    def rows(n, count, used=None):
+        return pl.ds(pl.multiple_of(n * count, count), used or count)
+
+    def drain(buf, count, sem):
+        part = buf.at[pl.ds(0, count)]
+        pltpu.make_async_copy(part, part, sem).wait()
 
     def tile(n):
         return slice(128 * n, 128 * n + 128)
@@ -306,8 +311,8 @@
     loads[10].wait()
     vt = mats[0].T
     next_vt = jnp.concatenate([vt[:, 1:], jnp.zeros((nz, 1), F32)], 1)
-    main = dot_nt(vt, rhs[0:256, :]) + dot_nt(vt - next_vt, iw)
-    extra = dot_nt(vt, rhs[256:416, :])
+    both = dot_nt(vt, rhs[...])
+    main, extra = both[:, :256] + dot_nt(vt - next_vt, iw), both[:, 256:]
     modal[0] = main[:, :128]
     modal[1] = main[:, 128:]
     modal[2] = jnp.concatenate([extra[:, :32], jnp.zeros((nz, 96), F32)], 1)
@@ -322,8 +327,6 @@
             s1[pl.ds(4, ng, stride=8), :] = jnp.where(lane_g < 32, even, roll(odd, 32))
         else:
             s1[pl.ds(5, ng, stride=8), :] = jnp.where((lane_g & 31) < 2, even, roll(odd, 2))
-            s1[pl.ds(6, ng, stride=8), :] = jnp.zeros((ng, 128), F32)
-            s1[pl.ds(7, ng, stride=8), :] = jnp.zeros((ng, 128), F32)
 
     @pl.when(owner)
     def _():
@@ -338,14 +341,14 @@
     def send1(to):
         @pl.when(has(to))
         def _():
-            remote(s1.at[rows(pair_of(to), 8)], r1.at[rows(t, 8)], s, to, p_send.at[0], p_recv.at[0]).start()
+            remote(s1.at[rows(pair_of(to), 8, 6)], r1.at[rows(t, 8, 6)], s, to, p_send.at[0], p_recv.at[0]).start()
 
     for i in range(nt - 1):
         send1(partner(t, i, nt))
 
     @pl.when(owner)
     def _():
-        pltpu.make_async_copy(s1.at[rows(mine, 8)], r1.at[rows(t, 8)], p_recv.at[0]).start()
+        pltpu.make_async_copy(s1.at[rows(mine, 8, 6)], r1.at[rows(t, 8, 6)], p_recv.at[0]).start()
 
     if late:
 
@@ -384,10 +387,11 @@
     halos[1].start()
     halos[3].start()
     loads[9].wait()
+    yfwd[...] = jnp.concatenate([table(2), table(3)], 1)
 
     @pl.when(owner)
     def _():
-        pltpu.make_async_copy(r1, r1, p_recv.at[0]).wait()
+        drain(r1, 6 * nt, p_recv.at[0])
         x = jnp.concatenate([r1[pl.ds(i, nt, stride=8), :] for i in range(5)], 1)
         y = dot(table(4), x)
         z = dot(table(5), r1[pl.ds(5, nt, stride=8), :])
@@ -398,13 +402,11 @@
             for i in range(4):
                 s2[pl.ds(4 * q + i, ns, stride=16), :] = parts[i][q * ns : (q + 1) * ns]
         s2[pl.ds(8, ns, stride=16), :] = jnp.where(at < 64, y[:ns, tile(4)], roll(y[ns:, tile(4)], 64))
-        for i in range(9, 16):
-            s2[pl.ds(i, ns, stride=16), :] = jnp.zeros((ns, 128), F32)
 
         for i in range(1, ns):
             j = lax.rem(s + i, ns)
-            remote(s2.at[rows(j, 16)], r2.at[rows(s, 16)], j, t, p_send.at[1], p_recv.at[1]).start()
-        pltpu.make_async_copy(s2.at[rows(s, 16)], r2.at[rows(s, 16)], p_recv.at[1]).start()
+            remote(s2.at[rows(j, 16, 9)], r2.at[rows(s, 16, 9)], j, t, p_send.at[1], p_recv.at[1]).start()
+        pltpu.make_async_copy(s2.at[rows(s, 16, 9)], r2.at[rows(s, 16, 9)], p_recv.at[1]).start()
 
     if late:
 
@@ -415,51 +417,7 @@
     halos[0].start()
     halos[2].start()
 
-    @pl.when(owner)
-    def _():
-        loads[8].wait()
-        pltpu.make_async_copy(r2, r2, p_recv.at[1]).wait()
-        part = [
-            jnp.concatenate([r2[pl.ds(2 * n + i, ns, stride=16), :] for i in range(2)], 0) for n in range(4)
-        ]
-        group = lax.broadcasted_iota(jnp.int32, (2 * ns, 128), 1) // 32
-        x = []
-        for r in range(4):
-            v = roll(part[0], -32 * r)
-            for n in range(1, 4):
-                v = jnp.where(group == n, roll(part[n], 32 * (n - r)), v)
-            x.append(v)
-        x = jnp.concatenate(x, 0)
-        y = dot(table(2), x) + dot(table(3), r2[pl.ds(8, ns, stride=16), :])
-        inner = spec[0:128, :]
-        y = dot(y, inner)
-        wide = lax.broadcasted_iota(jnp.int32, (1, 128), 1)
-        own = jnp.where((wide & 32) == 0, eig[2 * mine], eig[2 * mine + 1])
-        y = -y / (own + table(0) + spec[128:129, :])
-        y = dot(table(1), dot_nt(y, inner))
-        s3[...] = y
-
-        for i in range(1, ns):
-            j = lax.rem(s + i, ns)
-            remote(s3.at[rows(j, 16)], r3.at[rows(s, 16)], j, t, p_send.at[2], p_recv.at[2]).start()
-        pltpu.make_async_copy(s3.at[rows(s, 16)], r3.at[rows(s, 16)], p_recv.at[2]).start()
-
     diffusion = (0.0, 0.0, KAPPA, -KAPPA, 0.0, 0.0)
-    halos[0].wait_recv()
-    unpack_x(xfw, ((iw14, 1, -3, 0, 3), (it14, 1, -3, 3, 3), (iu10, 0, -1, 6, 1), (iv10, 0, -1, 7, 1), (u10, 0, -3, 8, 3), (c18, 2, -5, 11, 5)))
-    halos[2].wait_recv()
-    unpack_x(xfe, ((iw14, 1, 32, 0, 3), (it14, 1, 32, 3, 3), (iu10, 0, 32, 6, 1), (iv10, 0, 32, 7, 1), (u10, 0, 32, 8, 2), (c18, 2, 32, 11, 5)))
-
-    def x_faces(n, _):
-        at = pl.ds(pl.multiple_of(8 * n, 8), 8)
-        value, parts = weno_parts(c18[at, 256:896], u10[at, :], 1, lambda f: f)
-        wx[at, :] = DT * value
-        for o in range(6):
-            ax[o, at, :] = roll(DT * (parts[o] + diffusion[o]), o - 2)
-        return 0
-
-    lax.fori_loop(0, nz // 8, x_faces, 0)
-
     halos[1].wait_recv()
     halos[3].wait_recv()
     v = yfs2[5]
@@ -497,7 +455,52 @@
 
     @pl.when(owner)
     def _():
-        pltpu.make_async_copy(r3, r3, p_recv.at[2]).wait()
+        loads[8].wait()
+        loads[13].wait()
+        drain(r2, 9 * ns, p_recv.at[1])
+        part = [
+            jnp.concatenate([r2[pl.ds(2 * n + i, ns, stride=16), :] for i in range(2)], 0) for n in range(4)
+        ]
+        group = lax.broadcasted_iota(jnp.int32, (2 * ns, 128), 1) // 32
+        x = []
+        for r in range(4):
+            v = roll(part[0], -32 * r)
+            for n in range(1, 4):
+                v = jnp.where(group == n, roll(part[n], 32 * (n - r)), v)
+            x.append(v)
+        x.append(r2[pl.ds(8, ns, stride=16), :])
+        y = dot(yfwd[...], jnp.concatenate(x, 0))
+        inner = spec[0:128, :]
+        y = dot(y, inner)
+        wide = lax.broadcasted_iota(jnp.int32, (1, 128), 1)
+        own = jnp.where((wide & 32) == 0, eig[2 * mine], eig[2 * mine + 1])
+        y = -y / (own + table(0) + spec[128:129, :])
+        y = dot(table(1), dot_nt(y, inner))
+        s3[...] = y
+
+        for i in range(1, ns):
+            j = lax.rem(s + i, ns)
+            remote(s3.at[rows(j, 16, 14)], r3.at[rows(s, 16, 14)], j, t, p_send.at[2], p_recv.at[2]).start()
+        pltpu.make_async_copy(s3.at[rows(s, 16, 14)], r3.at[rows(s, 16, 14)], p_recv.at[2]).start()
+
+    halos[0].wait_recv()
+    unpack_x(xfw, ((iw14, 1, -3, 0, 3), (it14, 1, -3, 3, 3), (iu10, 0, -1, 6, 1), (iv10, 0, -1, 7, 1), (u10, 0, -3, 8, 3), (c18, 2, -5, 11, 5)))
+    halos[2].wait_recv()
+    unpack_x(xfe, ((iw14, 1, 32, 0, 3), (it14, 1, 32, 3, 3), (iu10, 0, 32, 6, 1), (iv10, 0, 32, 7, 1), (u10, 0, 32, 8, 2), (c18, 2, 32, 11, 5)))
+
+    def x_faces(n, _):
+        at = pl.ds(pl.multiple_of(8 * n, 8), 8)
+        value, parts = weno_parts(c18[at, 256:896], u10[at, :], 1, lambda f: f)
+        wx[at, :] = DT * value
+        for o in range(6):
+            ax[o, at, :] = roll(DT * (parts[o] + diffusion[o]), o - 2)
+        return 0
+
+    lax.fori_loop(0, nz // 8, x_faces, 0)
+
+    @pl.when(owner)
+    def _():
+        drain(r3, 14 * ns, p_recv.at[2])
         left = lax.broadcasted_iota(jnp.int32, (ns, 128), 1) < 64
         cols = []
         for i in range(7):
@@ -537,8 +540,8 @@
     w10[...] = iw + DT * NU * spread(iw)
     iu10[...] = iu10[...] + DT * NU * spread(iu10[...])
     iv10[...] = iv10[...] + DT * NU * spread(iv10[...])
-    loads[11].wait()
-    loads[12].wait()
+    for n in (11, 12):
+        loads[n].wait()
     vert[0] = jnp.concatenate([mats[1, pl.ds(0, ng, stride=2), :], mats[1, pl.ds(1, ng, stride=2), :]], 0).T
     vert[1] = mats[2].T
 
@@ -595,15 +598,15 @@
 
     @pl.when(owner)
     def _():
-        for n, buf, count in ((0, s1, 8 * (ng - 1)), (1, s2, 16 * (ns - 1)), (2, s3, 16 * (ns - 1)), (3, s4, 8 * (nt - 1))):
-            part = buf.at[pl.ds(0, count)]
-            pltpu.make_async_copy(part, part, p_send.at[n]).wait()
+        for n, buf, count in ((0, s1, 6 * (ng - 1)), (1, s2, 9 * (ns - 1)), (2, s3, 14 * (ns - 1)), (3, s4, 8 * (nt - 1))):
+            drain(buf, count, p_send.at[n])
 
     if late:
 
         @pl.when(other)
         def _():
-            pltpu.make_async_copy(s1, s1, p_send.at[0]).wait()
+            drain(s1, 6 * ng, p_send.at[0])
+            loads[13].wait()
             loads[8].wait()
 
 
@@ -626,7 +629,6 @@
     ng = nz // 2
     packed, spectral, places = consts
     vmem, anywhere = pl.BlockSpec(memory_space=pltpu.VMEM), pl.BlockSpec(memory_space=pl.ANY)
-    smem = pl.BlockSpec(memory_space=pltpu.SMEM)
 
     def buf(*shape):
         return pltpu.VMEM(shape, F32)
@@ -635,10 +637,10 @@
     made = pl.pallas_call(
         functools.partial(kernel, ns, nt, nz, places),
         out_shape=[pltpu.VMEM((nz, 640), F32)] * 4,
-        in_specs=[anywhere] * 11 + [smem] + [anywhere] * 2,
+        in_specs=[anywhere] * 14,
         out_specs=[vmem] * 4,
         scratch_shapes=[
-            buf(8, 10, 64, nz), buf(3, nz, nz), buf(*packed.shape), buf(136, 128), buf(416, nz),
+            pltpu.SMEM((nz,), F32), buf(8, 10, 64, nz), buf(3, nz, nz), buf(*packed.shape), buf(136, 128), buf(416, nz),
             buf(nz, 640), buf(nz, 896), buf(nz, 640), buf(nz, 1152),
             buf(nz, 640), buf(nz, 640), buf(nz, 896), buf(nz, 896), buf(8, nz, 128),
             buf(nz, 128), buf(nz, 128), buf(nz, 128), buf(nz, 128),
@@ -646,8 +648,8 @@
             buf(8 * ng, 128), buf(8 * nt, 128), buf(16 * ns, 128), buf(16 * ns, 128),
             buf(16 * ns, 128), buf(16 * ns, 128), buf(8 * nt, 128), buf(8 * ng, 128),
             buf(6, nz, 640), buf(nz, 640), buf(6, nz, 640), buf(nz, 640), buf(2, nz, 640),
-            buf(nz, 896), buf(2, nz, nz),
-            pltpu.SemaphoreType.DMA((13,)), pltpu.SemaphoreType.DMA((4,)), pltpu.SemaphoreType.DMA((4,)),
+            buf(nz, 896), buf(2, nz, nz), buf(ROWS * ns, ROWS * ns + ns),
+            pltpu.SemaphoreType.DMA((14,)), pltpu.SemaphoreType.DMA((4,)), pltpu.SemaphoreType.DMA((4,)),
             pltpu.SemaphoreType.DMA((4,)), pltpu.SemaphoreType.DMA((4,)), pltpu.SemaphoreType.REGULAR,
         ],
         compiler_params=pltpu.CompilerParams(

time: 47.7 us -> 45.5 us (0.954)
  Pallas kernels: 46.9 us -> 44.7 us
    pallas_call x1, Pallas kernels: 45.9 us -> 43.7 us  [call(): pl.pallas_call(functools.partial(kernel, ns, nt, nz, places), out_shape=[...]
where the time goes in v5:
time: 45.5 us; the launch traced here: 45.4 us
  Pallas kernels  44.7 us (98%)
  between operations  0.64 us (1%)
    pallas_call x1, Pallas kernels, call(): pl.pallas_call(functools.partial(kernel, ns, nt, nz, places), out_shape=[...  43.7 us
    pallas_call x1, Pallas kernels, call(): pl.pallas_call(finish, out_shape=[out] * 4, in_specs=[vmem] * 4, out_spec...  1.01 us

profile of v5, /device:TPU:1, one launch (start us, length us, event | category | flops | bytes accessed | tf_op | source)
XLA Modules:
  0.0 45.4 jit_solution(6438374165720691731)
XLA Ops:
  0.6 43.7 %shard_map.165 = (f32[48,640]{1,0:T(8,128)S(1)}, f32[48,640]{1,0:T(8,128)S(1)}, f32[48,640]{1,0:T(8,128)S(1)}, f32[48,640]{1,0:T(8,128)S(1)}) custom-call(f32[8,32,48]{2,1,0:T(8,128)} %bitcast.12, f32[8,32,48]{2,1,0:T(8,128)} %bitcast.13, f32[8,32,48]{2,1,0:T(8,128)} %bitcast.14, f32[8,32,48]{2,1,0:T(8,128)} %bitcast.15, f32[8,32,48]{2,1,0:T(8,128)} %bitcast.16, ...), custom_call_target="tpu_custom_call" | custom-call | tf_op jit(solution)/shard_map/pallas_call | solution.py:637
  44.4 1.0 %shard_map.166 = (f32[8,32,48]{2,1,0:T(8,128)}, f32[8,32,48]{2,1,0:T(8,128)}, f32[8,32,48]{2,1,0:T(8,128)}, f32[8,32,48]{2,1,0:T(8,128)}) custom-call(f32[48,640]{1,0:T(8,128)S(1)} %get-tuple-element.12.a, f32[48,640]{1,0:T(8,128)S(1)} %get-tuple-element.13.b, f32[48,640]{1,0:T(8,128)S(1)} %get-tuple-element.14.c, f32[48,640]{1,0:T(8,128)S(1)} %get-tuple-element.15.d), custom_call_target="tpu_custom_call" | custom-call | tf_op jit(solution)/shard_map/pallas_call | solution.py:659

commit v6 on v5

--- a/solution.py
+++ b/solution.py
@@ -392,9 +392,9 @@
     @pl.when(owner)
     def _():
         drain(r1, 6 * nt, p_recv.at[0])
-        x = jnp.concatenate([r1[pl.ds(i, nt, stride=8), :] for i in range(5)], 1)
-        y = dot(table(4), x)
-        z = dot(table(5), r1[pl.ds(5, nt, stride=8), :])
+        x = jnp.concatenate([r1[pl.ds(i, nt, stride=8), :] for i in range(6)], 1)
+        both = dot(packed[places[4][0] : places[5][1], :nt], x)
+        y, z = both[:nt], both[nt:, tile(5)]
         first = (lax.broadcasted_iota(jnp.int32, (nt, 128), 1) & 31) == 0
         at = lax.broadcasted_iota(jnp.int32, (ns, 128), 1)
         parts = [y[:, tile(i)] + jnp.where(first, roll(z, -i), 0.0) for i in range(4)]
@@ -619,8 +619,11 @@
                 made[n, 2 * k - 1] = v[8:40]
             if k < 4:
                 made[n, 2 * k] = v[72:104]
-        copies.append(pltpu.make_async_copy(made.at[n], dst, sem.at[n]))
-        copies[n].start()
+            if k in (2, 4):
+                part = pl.ds(2 * (k - 2), 4)
+                copy = pltpu.make_async_copy(made.at[n, part], dst.at[part], sem.at[n, k // 2 - 1])
+                copy.start()
+                copies.append(copy)
     for copy in copies:
         copy.wait()
 
@@ -661,7 +664,7 @@
         out_shape=[out] * 4,
         in_specs=[vmem] * 4,
         out_specs=[anywhere] * 4,
-        scratch_shapes=[buf(4, ROWS, COLS, nz), pltpu.SemaphoreType.DMA((4,))],
+        scratch_shapes=[buf(4, ROWS, COLS, nz), pltpu.SemaphoreType.DMA((4, 2))],
     )(*[pltpu.with_memory_space_constraint(v, pltpu.VMEM) for v in made])
 
 

time: 45.5 us -> 45.6 us (level)
  no operation moved by 1% of the time
where the time goes in v6:
time: 45.6 us; the launch traced here: 45.5 us
  Pallas kernels  44.8 us (98%)
  between operations  0.64 us (1%)
    pallas_call x1, Pallas kernels, call(): pl.pallas_call(functools.partial(kernel, ns, nt, nz, places), out_shape=[...  43.8 us
    pallas_call x1, Pallas kernels, call(): pl.pallas_call(finish, out_shape=[out] * 4, in_specs=[vmem] * 4, out_spec...  1.03 us

profile of v6, /device:TPU:1, one launch (start us, length us, event | category | flops | bytes accessed | tf_op | source)
XLA Modules:
  0.0 45.5 jit_solution(5431340287170034087)
XLA Ops:
  0.6 43.8 %shard_map.165 = (f32[48,640]{1,0:T(8,128)S(1)}, f32[48,640]{1,0:T(8,128)S(1)}, f32[48,640]{1,0:T(8,128)S(1)}, f32[48,640]{1,0:T(8,128)S(1)}) custom-call(f32[8,32,48]{2,1,0:T(8,128)} %bitcast.12, f32[8,32,48]{2,1,0:T(8,128)} %bitcast.13, f32[8,32,48]{2,1,0:T(8,128)} %bitcast.14, f32[8,32,48]{2,1,0:T(8,128)} %bitcast.15, f32[8,32,48]{2,1,0:T(8,128)} %bitcast.16, ...), custom_call_target="tpu_custom_call" | custom-call | tf_op jit(solution)/shard_map/pallas_call | solution.py:640
  44.5 1.0 %shard_map.166 = (f32[8,32,48]{2,1,0:T(8,128)}, f32[8,32,48]{2,1,0:T(8,128)}, f32[8,32,48]{2,1,0:T(8,128)}, f32[8,32,48]{2,1,0:T(8,128)}) custom-call(f32[48,640]{1,0:T(8,128)S(1)} %get-tuple-element.12.a, f32[48,640]{1,0:T(8,128)S(1)} %get-tuple-element.13.b, f32[48,640]{1,0:T(8,128)S(1)} %get-tuple-element.14.c, f32[48,640]{1,0:T(8,128)S(1)} %get-tuple-element.15.d), custom_call_target="tpu_custom_call" | custom-call | tf_op jit(solution)/shard_map/pallas_call | solution.py:662
